TPU v7x, 128 devices: a whole 4x4x4 slice. The times are simulated.
128 devices in a mesh: seq: 16 (over x, y_lo, core), tp: 8 (over z, y_hi).
Axes of the slice: x: 4, y: 4 (y_hi: 2, y_lo: 2; y = y_hi * 2 + y_lo), z: 4, core: 2. Of those that a mesh axis runs over, the one named last changes fastest.
Arguments:
- item_states: bfloat16 [32768, 2048], P(('seq', 'tp')), may hold values from -6 to 6
- item_gain: float32 [2048], replicated, may hold values from 0.1 to 1.9
- adapter: bfloat16 [2048, 4096], P(('seq', 'tp')), may hold values from -0.125 to 0.125
- send_rows: int32 [16, 128, 4], P(None, ('seq', 'tp')), may hold values from 0 to 255, as said below
- hist_slot: int32 [16384], P('seq'), may hold values from 0 to 511
- hist_lengths: int32 [4], replicated, may hold values from 1 to 12288, 16384 in all
- user_gain: float32 [4096], replicated, may hold values from 0.1 to 1.9
- w_query: bfloat16 [4096, 2048], P(None, 'tp')
- w_key: bfloat16 [4096, 2048], P(None, 'tp')
- w_value: bfloat16 [4096, 2048], P(None, 'tp'), may hold values from -0.09375 to 0.09375
Outputs:
- attended: bfloat16 [16384, 2048], P('seq', 'tp')
Inputs may be any that keep to these rules, and one draw needn't show every extreme that they name: Within each block send_rows[s, r, :] the 4 entries are distinct rows of device r's 256 items. `hist_slot`: slot r * 4 + c names the c-th row that device r sends to the position's seq index. `hist_lengths`: they sum to 16384.
All inputs are finite; a program needn't handle non-finite values.
Results may differ from a plain program's by a relative error of at most 0.012.
Values may be sent and summed in bfloat16 or wider, within the bound.
A program may use at most 128 MiB of HBM per device.

v0:
```python
import math

import jax
import jax.numpy as jnp
from jax import lax
from jax.sharding import PartitionSpec as P

HD = 128


def normed(values, gain):
    wide = values.astype(jnp.float32)
    factor = lax.rsqrt(jnp.mean(wide * wide, axis=-1, keepdims=True) + 1e-05)
    return (wide * factor * gain).astype(jnp.bfloat16)


def encode(left, adapter):
    total = jnp.dot(
        left,
        lax.all_gather(adapter, ("seq", "tp"), axis=0, tiled=True),
        preferred_element_type=jnp.float32,
    )
    return total.astype(jnp.bfloat16)


def per_device(
    item_states,
    item_gain,
    adapter,
    send_rows,
    hist_slot,
    hist_lengths,
    user_gain,
    w_query,
    w_key,
    w_value,
):
    ntp = lax.axis_size("tp")
    nseq = lax.axis_size("seq")
    width = adapter.shape[1]
    item_norm = normed(item_states, item_gain)
    picks = send_rows[:, 0, :]
    slots_out = picks.shape[1]
    flat_picks = picks.reshape(-1)
    chosen_norm = jnp.take(item_norm, flat_picks, axis=0)
    chosen_emb = encode(chosen_norm, adapter)
    chosen = chosen_emb.reshape(nseq, 1, slots_out, width)
    copies = jnp.broadcast_to(chosen, (nseq, ntp, slots_out, width)).reshape(
        nseq * ntp, slots_out, width
    )
    arrived = lax.all_to_all(copies, ("seq", "tp"), split_axis=0, concat_axis=0, tiled=True)
    received = arrived.reshape(-1, width)
    history = jnp.take(received, hist_slot, axis=0)
    hist_norm = normed(history, user_gain)
    query = jnp.dot(hist_norm, w_query, preferred_element_type=jnp.float32).astype(jnp.bfloat16)
    keys_local = jnp.dot(hist_norm, w_key, preferred_element_type=jnp.float32).astype(jnp.bfloat16)
    values_local = jnp.dot(hist_norm, w_value, preferred_element_type=jnp.float32).astype(
        jnp.bfloat16
    )
    rows_here = query.shape[0]
    heads_here = query.shape[1] // HD
    scale = 1.0 / math.sqrt(HD)
    ends = jnp.cumsum(hist_lengths)
    first_pos = lax.axis_index("seq") * rows_here
    qpos = first_pos + jnp.arange(rows_here, dtype=jnp.int32)
    quser = jnp.sum((qpos[:, None] >= ends[None, :]).astype(jnp.int32), axis=1)
    qheads = query.reshape(rows_here, heads_here, HD)
    init = (
        jnp.full((heads_here, rows_here), -1e30, jnp.float32),
        jnp.zeros((heads_here, rows_here), jnp.float32),
        jnp.zeros((heads_here, rows_here, HD), jnp.float32),
    )
    kpiece = lax.all_gather(keys_local, "seq", axis=0, tiled=True)
    vpiece = lax.all_gather(values_local, "seq", axis=0, tiled=True)
    rows = kpiece.shape[0]
    block = math.gcd(rows, 1024)

    def step(index, state):
        offset = index * block
        kpos = offset + jnp.arange(block, dtype=jnp.int32)
        largest, total, accum = state
        kblock = lax.dynamic_slice_in_dim(kpiece, offset, block, 0).reshape(block, heads_here, HD)
        vblock = lax.dynamic_slice_in_dim(vpiece, offset, block, 0).reshape(block, heads_here, HD)
        kuser = jnp.sum((kpos[:, None] >= ends[None, :]).astype(jnp.int32), axis=1)
        scores = (
            jnp.einsum("qhd,khd->hqk", qheads, kblock, preferred_element_type=jnp.float32) * scale
        )
        allowed = (kpos[None, :] <= qpos[:, None]) & (kuser[None, :] == quser[:, None])
        scores = jnp.where(allowed[None], scores, jnp.float32(-1e30))
        newest = jnp.maximum(largest, jnp.max(scores, axis=2))
        shrink = jnp.exp(largest - newest)
        prob = jnp.where(allowed[None], jnp.exp(scores - newest[:, :, None]), jnp.float32(0.0))
        total = total * shrink + jnp.sum(prob, axis=2)
        accum = accum * shrink[:, :, None] + jnp.einsum(
            "hqk,khd->hqd", prob.astype(jnp.bfloat16), vblock, preferred_element_type=jnp.float32
        )
        return (newest, total, accum)

    largest, total, accum = lax.fori_loop(0, rows // block, step, init)
    result = accum / total[:, :, None]
    return jnp.transpose(result, (1, 0, 2)).reshape(rows_here, heads_here * HD).astype(jnp.bfloat16)


def solution(mesh):
    in_specs = (
        P(("seq", "tp"), None),
        P(),
        P(("seq", "tp"), None),
        P(None, ("seq", "tp"), None),
        P("seq"),
        P(),
        P(),
        P(None, "tp"),
        P(None, "tp"),
        P(None, "tp"),
    )
    out_specs = P("seq", "tp")
    return jax.shard_map(
        per_device, mesh=mesh, in_specs=in_specs, out_specs=out_specs, check_vma=False
    )
```

profile of v0, /device:TPU:6, one launch (start us, length us, event | category | flops | bytes accessed | tf_op | source)
XLA Modules:
  0.0 760.3 jit_solution(1737927780583824766)
XLA Ops:
  12.0 324.4 %all-gather.4.cloned.1.call-done = bf16[2048,4096]{1,0:T(8,128)(2,1)} async-done(((bf16[16,4096]{1,0:T(8,128)(2,1)}), bf16[2048,4096]{1,0:T(8,128)(2,1)}) %all-gather.4.cloned.1.call-update) | async-done | bytes 16777232 | tf_op jit(solution)/shard_map/all_gather | solution.py:20
  336.4 8.9 %convolution_convert_fusion = bf16[64,4096]{1,0:T(8,128)(2,1)S(1)} fusion(bf16[2048,4096]{1,0:T(8,128)(2,1)} %all-gather.4.cloned.1.call-done, bf16[64,2048]{1,0:T(8,128)(2,1)S(1)} %gather_fusion, pred[64]{0:T(512)(128)(4,1)S(1)} %compare_and_fusion.2), kind=kOutput, calls=%fused_computation.32 | convolution fusion | flops 1074135040 | bytes 17563712 | tf_op jit(solution)/shard_map/dot_general | solution.py:18
  345.5 4.1 broadcast_in_dim.116
  349.6 11.0 %all-to-all-start = ((bf16[128,4,4096]{2,1,0:T(4,128)(2,1)}), bf16[128,4,4096]{2,1,0:T(4,128)(2,1)}, u32[]{:S(2)}, u32[]{:S(2)}) async-start(bf16[128,4,4096]{2,1,0:T(4,128)(2,1)} %bitcast.57), calls=%async_computation | async-start | bytes 8388608 | tf_op jit(solution)/shard_map/all_to_all | solution.py:51
  360.8 50.8 %all-to-all-done = bf16[128,4,4096]{2,1,0:T(4,128)(2,1)} async-done(((bf16[128,4,4096]{2,1,0:T(4,128)(2,1)}), bf16[128,4,4096]{2,1,0:T(4,128)(2,1)}, u32[]{:S(2)}, u32[]{:S(2)}) %all-to-all-start) | async-done | bytes 4194336 | tf_op jit(solution)/shard_map/all_to_all | solution.py:51
  411.7 6.9 reshape.182
  418.6 17.8 %gather_fusion.1 = bf16[1024,4096]{1,0:T(8,128)(2,1)} fusion(bf16[512,4096]{1,0:T(8,128)(2,1)} %reshape.182, s32[1024]{0:T(1024)S(1)} %fusion.26), kind=kCustom, calls=%fused_computation.1 | custom fusion | bytes 16781312 | tf_op jit(solution)/shard_map/jit(_take)/gather | solution.py:53
  436.4 5.9 fusion.16
  442.3 4.4 fusion.18
  453.3 7.3 convolution_convert_fusion.3
  460.9 5.8 convolution_convert_fusion.2
  467.0 36.2 %all-gather.8.cloned.1.call-done = bf16[16384,256]{1,0:T(8,128)(2,1)} async-done(((bf16[1024,256]{1,0:T(8,128)(2,1)}), bf16[16384,256]{1,0:T(8,128)(2,1)}) %all-gather.8.cloned.1.call-update) | async-done | bytes 8388624 | tf_op jit(solution)/shard_map/all_gather | solution.py:74
  503.2 54.7 %all-gather.6.cloned.1.call-done = bf16[16384,256]{1,0:T(8,128)(2,1)} async-done(((bf16[1024,256]{1,0:T(8,128)(2,1)}), bf16[16384,256]{1,0:T(8,128)(2,1)}) %all-gather.6.cloned.1.call-update) | async-done | bytes 8388624 | tf_op jit(solution)/shard_map/all_gather | solution.py:73
  557.9 193.3 %while.18 = (s32[]{:T(128)}, f32[2,1024]{1,0:T(2,128)S(1)}, f32[2,1024]{1,0:T(2,128)S(1)}, f32[2,1024,128]{2,1,0:T(8,128)}, s32[4]{0:T(128)S(1)}, /*index=5*/s32...) while((s32[]{:T(128)}, f32[2,1024]{1,0:T(2,128)S(1)}, ...), condition=%wide.region_8.9_spmd.clone, body=%wide.region_4.8_spmd.clone.sunk | while | flops 1104960512 | bytes 45777176 | solution.py:99
  577.3 3.7 fusion.57
  589.4 3.7 fusion.57
  613.6 3.7 fusion.57
  625.6 3.7 fusion.57
  649.8 3.7 fusion.57
  661.9 3.7 fusion.57
  686.1 3.7 fusion.57
  698.1 3.7 fusion.57
  722.3 3.7 fusion.57
  734.4 3.7 fusion.57
  (291 shorter events, 170.3 us)
Async XLA Ops:
  6.5 443.4 %copy-start = (bf16[4096,256]{1,0:T(8,128)(2,1)S(1)}, bf16[4096,256]{1,0:T(8,128)(2,1)}, u32[]{:S(2)}) copy-start(bf16[4096,256]{1,0:T(8,128)(2,1)} %param.21) | copy-start | bytes 6291460
  6.5 329.9 %all-gather.4.cloned.1.call-start = ((), (), s32[]{:S(2)}) async-start(), calls=%async_computation.1 | async-start | bytes 16908288 | tf_op jit(solution)/shard_map/all_gather | solution.py:20
  345.3 15.5 %copy-start.6 = (s32[1024]{0:T(1024)S(1)}, s32[1024]{0:T(1024)}, u32[]{:S(2)}) copy-start(s32[1024]{0:T(1024)} %param.16) | copy-start | bytes 12292
  349.6 62.1 %all-to-all-start = ((bf16[128,4,4096]{2,1,0:T(4,128)(2,1)}), bf16[128,4,4096]{2,1,0:T(4,128)(2,1)}, u32[]{:S(2)}, u32[]{:S(2)}) async-start(bf16[128,4,4096]{2,1,0:T(4,128)(2,1)} %bitcast.57), calls=%async_computation | async-start | bytes 8388608 | tf_op jit(solution)/shard_map/all_to_all | solution.py:51
  360.6 142.6 %all-gather.8.cloned.1.call-start = ((), (), s32[]{:S(2)}) async-start(), calls=%async_computation.3 | async-start | bytes 8912896 | tf_op jit(solution)/shard_map/all_gather | solution.py:74
  418.6 23.7 %copy-start.7 = (f32[4096]{0:T(1024)S(1)}, f32[4096]{0:T(1024)}, u32[]{:S(2)}) copy-start(f32[4096]{0:T(1024)} %param.18) | copy-start | bytes 49156
  436.4 5.9 copy-start.2
  453.0 7.6 %copy-start.9 = (s32[4]{0:T(128)S(1)}, s32[4]{0:T(128)}, u32[]{:S(2)}) copy-start(s32[4]{0:T(128)} %param.17) | copy-start | bytes 52
  453.0 7.9 %copy-start.8 = (bf16[4096,256]{1,0:T(8,128)(2,1)S(1)}, bf16[4096,256]{1,0:T(8,128)(2,1)}, u32[]{:S(2)}) copy-start(bf16[4096,256]{1,0:T(8,128)(2,1)} %param.19) | copy-start | bytes 6291460
  453.1 104.9 %all-gather.6.cloned.1.call-start = ((), (), s32[]{:S(2)}) async-start(), calls=%async_computation.2 | async-start | bytes 8912896 | tf_op jit(solution)/shard_map/all_gather | solution.py:73
  560.9 4.3 copy-start.4
  573.0 4.3 copy-start.4
  585.1 4.3 copy-start.4
  597.2 4.3 copy-start.4
  609.3 4.3 copy-start.4
  633.4 4.3 copy-start.4
  645.5 4.3 copy-start.4
  657.6 4.3 copy-start.4
  669.7 4.3 copy-start.4
  681.8 4.3 copy-start.4
  693.8 4.3 copy-start.4
  705.9 4.3 copy-start.4
  718.0 4.3 copy-start.4
  742.2 4.3 copy-start.4
  (20 other events, 31.0 us)
Sparse Core Ops, SparseCore 0:
  9.0 327.3 all-gather.3
  453.2 49.9 all-gather.7
  504.9 52.9 all-gather.5
where the time goes:
time: 763 us; the launch traced here: 760 us
  waiting for transfers between devices  467 us (61%)
  matrix products  116 us (15%)
  local copies, waits for them, and re-layouts  77.6 us (10%)
  other arithmetic  73.3 us (10%)
  between operations  13.3 us (2%)
  starting transfers between devices  11.5 us (2%)
    all_gather x1, waiting for transfers between devices, encode(): lax.all_gather(adapter, ('seq', 'tp'), axis=0, tiled=True)  324 us
    dot_general x16, matrix products, step(): jnp.einsum('hqk,khd->hqd', prob.astype(jnp.bfloat16), vblock, preferred_e...  59.8 us
    all_gather x1, waiting for transfers between devices, per_device(): kpiece = lax.all_gather(keys_local, 'seq', axis=0, tiled=True)  54.7 us
    all_to_all x1, waiting for transfers between devices, per_device(): lax.all_to_all(copies, ('seq', 'tp'), split_axis=0, concat_axis=0, tiled=...  50.8 us
    all_gather x1, waiting for transfers between devices, per_device(): vpiece = lax.all_gather(values_local, 'seq', axis=0, tiled=True)  36.2 us
    reduce_sum x16, other arithmetic, step(): total = total * shrink + jnp.sum(prob, axis=2)  36.1 us
    dot_general x16, matrix products, step(): jnp.einsum('qhd,khd->hqk', qheads, kblock, preferred_element_type=jnp.flo...  31.6 us
    dynamic_slice x32, local copies, waits for them, and re-layouts, step(): lax.dynamic_slice_in_dim(vpiece, offset, block, 0)  23.7 us
  transfers between devices with their start and end apart: 4, of which 4 were waited for; matrix products, arithmetic and copies ran while one was open for 2% of the time, Pallas kernels for 0%

commit v1 on v0

v1 whole, which is shorter than its diff:
```python
import math

import jax
import jax.numpy as jnp
from jax import lax
from jax.experimental import pallas as pl
from jax.experimental.pallas import tpu as pltpu
from jax.sharding import PartitionSpec as P

MESH = pl.DeviceIdType.MESH
HD = 128
USERS = 4
EPS = 1e-05
LOG2E = 1.4426950408889634
EMPTY = -1e30
FLOOR = -1e25
BF = jnp.bfloat16
F32 = jnp.float32


def dot(a, b):
    return jnp.dot(a, b, preferred_element_type=F32)


class Group:
    def __init__(self, axis):
        s, t = lax.axis_index("seq"), lax.axis_index("tp")
        if axis == "seq":
            ring, pair, core = s // 4, (s // 2) % 2, s % 2
            self.block = lambda dr=0, dp=0, ds=0: (
                ((ring + dr) % 4) * 4 + ((pair + dp) % 2) * 2 + (core + ds) % 2
            )
            self.device = lambda *d: (self.block(*d), t)
            self.cores = True
        else:
            ring, pair = t // 2, t % 2
            self.block = lambda dr=0, dp=0: ((ring + dr) % 4) * 2 + (pair + dp) % 2
            self.device = lambda *d: (s, self.block(*d))
            self.cores = False
        self.right, self.left, self.pair = self.device(1, 0), self.device(3, 0), self.device(0, 1)
        self.sib = self.device(0, 0, 1) if self.cores else None


class Gather:
    def __init__(self, group, buf, half, send, recv):
        self.g, self.buf, self.half, self.send, self.recv = group, buf, half, send, recv
        self.count, self.sent = 0, []

    def view(self, index, part=None):
        ref = self.buf.at[index]
        if part is None:
            return ref
        axis, cut, end = self.half
        piece = pl.ds(0, cut) if part == 0 else pl.ds(cut, end - cut)
        return ref.at[(slice(None),) * axis + (piece,)]

    def push(self, index, device, slot, part=None):
        ref = self.view(index, part)
        copy = pltpu.make_async_remote_copy(
            src_ref=ref,
            dst_ref=ref,
            send_sem=self.send.at[self.count],
            recv_sem=self.recv.at[slot],
            device_id=device,
            device_id_type=MESH,
        )
        copy.start()
        self.count += 1
        self.sent.append(copy)

    def got(self, index, slot, part=None):
        ref = self.view(index, part)
        pltpu.make_async_remote_copy(
            src_ref=ref,
            dst_ref=ref,
            send_sem=self.send.at[0],
            recv_sem=self.recv.at[slot],
            device_id=self.g.right,
            device_id_type=MESH,
        ).wait_recv()

    def finish(self):
        for copy in self.sent:
            copy.wait_send()


class PairFirst(Gather):
    def start(self):
        g = self.g
        own = g.block()
        self.push(own, g.pair, 0)
        self.push(own, g.right, 1)
        self.push(own, g.left, 3)
        if g.cores:
            self.push(own, g.sib, 9)

    def from_pair(self):
        g = self.g
        block = g.block(0, 1)
        self.got(block, 0)
        self.push(block, g.right, 2)
        self.push(block, g.left, 4)
        if g.cores:
            self.push(block, g.sib, 10)

    def from_ring(self):
        g = self.g
        for dp in (0, 1):
            block = g.block(3, dp)
            self.got(block, 1 + dp)
            self.push(block, g.right, 5 + dp, 0)
            if g.cores:
                self.push(block, g.sib, 11 + dp)
            block = g.block(1, dp)
            self.got(block, 3 + dp)
            self.push(block, g.left, 7 + dp, 1)
            if g.cores:
                self.push(block, g.sib, 13 + dp)

    def from_far(self):
        g = self.g
        for dp in (0, 1):
            block = g.block(2, dp)
            self.got(block, 5 + dp, 0)
            self.got(block, 7 + dp, 1)
            if g.cores:
                self.push(block, g.sib, 15 + dp)

    def sib_own(self):
        for dp in (0, 1):
            self.got(self.g.block(0, dp, 1), 9 + dp)

    def sib_ring(self):
        for dp in (0, 1):
            self.got(self.g.block(3, dp, 1), 11 + dp)
            self.got(self.g.block(1, dp, 1), 13 + dp)

    def sib_far(self):
        for dp in (0, 1):
            self.got(self.g.block(2, dp, 1), 15 + dp)


class RingFirst(Gather):
    def start(self):
        g = self.g
        own = g.block()
        self.push(own, g.right, 1)
        self.push(own, g.left, 2)
        self.push(own, g.pair, 0)
        self.push(own, g.sib, 8)

    def from_pair(self):
        block = self.g.block(0, 1)
        self.got(block, 0)
        self.push(block, self.g.sib, 9)

    def from_ring(self):
        g = self.g
        block = g.block(3, 0)
        self.got(block, 1)
        self.push(block, g.right, 3, 0)
        self.push(block, g.pair, 5)
        self.push(block, g.sib, 10)
        block = g.block(1, 0)
        self.got(block, 2)
        self.push(block, g.left, 4, 1)
        self.push(block, g.pair, 6)
        self.push(block, g.sib, 11)

    def from_far(self):
        g = self.g
        block = g.block(2, 0)
        self.got(block, 3, 0)
        self.got(block, 4, 1)
        self.push(block, g.pair, 7)
        self.push(block, g.sib, 12)

    def pair_ring(self):
        g = self.g
        block = g.block(3, 1)
        self.got(block, 5)
        self.push(block, g.sib, 13)
        block = g.block(1, 1)
        self.got(block, 6)
        self.push(block, g.sib, 14)

    def pair_far(self):
        g = self.g
        block = g.block(2, 1)
        self.got(block, 7)
        self.push(block, g.sib, 15)

    def sib_own(self):
        g = self.g
        self.got(g.block(0, 0, 1), 8)
        self.got(g.block(0, 1, 1), 9)

    def sib_ring(self):
        g = self.g
        self.got(g.block(3, 0, 1), 10)
        self.got(g.block(1, 0, 1), 11)
        self.got(g.block(3, 1, 1), 13)
        self.got(g.block(1, 1, 1), 14)

    def sib_far(self):
        g = self.g
        self.got(g.block(2, 0, 1), 12)
        self.got(g.block(2, 1, 1), 15)


def pieces(values):
    first = values.astype(BF).astype(F32)
    second = (values - first).astype(BF).astype(F32)
    return first, second, values - first - second


def kernel(
    lengths,
    items,
    item_gain,
    adapter,
    picks,
    slot_row,
    slot_col,
    user_gain,
    w_query,
    w_key,
    w_value,
    out,
    abuf,
    scaled,
    weights,
    spread,
    xs,
    xa,
    xb,
    rows,
    mix,
    ebuf,
    raw,
    sums,
    query,
    kt,
    val,
    place,
    place_t,
    qpos,
    kpos_t,
    vpos,
    near,
    near_log,
    top,
    accum,
    w_sem,
    a_send,
    a_recv,
    r_send,
    r_recv,
    x_send,
    x_recv,
    m_send,
    m_recv,
    e_send,
    e_recv,
    s_send,
    s_recv,
    k_send,
    k_recv,
    v_send,
    v_recv,
):
    seq, tp = lax.axis_index("seq"), lax.axis_index("tp")
    nseq, ntp = lax.axis_size("seq"), lax.axis_size("tp")
    wide = adapter.shape[1]
    nslot, ditem = rows.shape
    chunks = ditem // HD
    ecols = ebuf.shape[2]
    hcols = w_query.shape[1]
    heads = hcols // HD
    npos = out.shape[0]
    nchosen = xs.shape[0]
    cap = nchosen // nseq
    first_pos = seq * npos

    loads = []
    for i, ref in enumerate((w_query, w_key, w_value)):
        load = pltpu.make_async_copy(ref, weights.at[i], w_sem.at[i])
        load.start()
        loads.append(load)

    barrier = pltpu.get_barrier_semaphore()
    for k in range(1, ntp):
        peer = (seq, lax.rem(tp + k, ntp))
        pl.semaphore_signal(barrier, inc=1, device_id=peer, device_id_type=MESH)
    for k in range(1, nseq):
        peer = (lax.rem(seq + k, nseq), tp)
        pl.semaphore_signal(barrier, inc=1, device_id=peer, device_id_type=MESH)

    pick = (lax.broadcasted_iota(jnp.int32, (nchosen, items.shape[0]), 1) == picks[...]).astype(BF)
    chosen = dot(pick, items[...])
    factor = lax.rsqrt(jnp.mean(chosen * chosen, axis=1, keepdims=True) + EPS)
    chosen = chosen * factor * item_gain[...]
    for k in range(chunks):
        spread[pl.ds(k, nchosen, stride=chunks), :] = chosen[:, k * HD : (k + 1) * HD]
    xs[...] = spread[: nchosen * chunks].reshape(nchosen, chunks, HD).astype(BF)

    pl.semaphore_wait(barrier, ntp + nseq - 2)

    over_tp, over_seq = Group("tp"), Group("seq")

    abuf[tp] = adapter[...]
    ga = PairFirst(over_tp, abuf, (1, wide // 2, wide), a_send, a_recv)
    ga.start()
    routed = []
    for k in range(1, nseq):
        peer = lax.rem(seq + k, nseq)
        copy = pltpu.make_async_remote_copy(
            src_ref=xs.at[pl.ds(peer * cap, cap)],
            dst_ref=xa.at[seq],
            send_sem=r_send.at[k],
            recv_sem=r_recv.at[k],
            device_id=(peer, tp),
            device_id_type=MESH,
        )
        copy.start()
        routed.append(copy)
    xa[seq] = xs[pl.ds(seq * cap, cap)]

    ends = [lengths[0]]
    for u in range(1, USERS):
        ends.append(ends[-1] + lengths[u])
    row_pos = lax.broadcasted_iota(jnp.int32, (1, npos), 1) + first_pos
    col_pos = lax.broadcasted_iota(jnp.int32, (npos, 1), 0) + first_pos

    def user_of(pos):
        total = jnp.zeros_like(pos)
        for end in ends:
            total = total + jnp.where(pos >= end, 1, 0)
        return total

    begin = jnp.zeros_like(col_pos)
    for end in ends:
        begin = jnp.maximum(begin, jnp.where(col_pos >= end, end, 0))
    place[...] = (lax.broadcasted_iota(jnp.int32, (npos, nslot), 1) == slot_col[...]).astype(BF)
    place_t[...] = (lax.broadcasted_iota(jnp.int32, (nslot, npos), 0) == slot_row[...]).astype(BF)
    belongs = lax.broadcasted_iota(jnp.int32, (16, npos), 0) % USERS == user_of(row_pos)
    held = dot(belongs.astype(BF), place[...])
    weigh = jnp.where(held > 0.5, jnp.log(jnp.maximum(held, 1.0)) * LOG2E, EMPTY)
    parts = pieces(weigh)
    part = lax.broadcasted_iota(jnp.int32, (16, nslot), 0) // USERS
    weigh = jnp.where(part == 0, parts[0], jnp.where(part == 1, parts[1], jnp.where(part == 2, parts[2], 0.0)))
    kt[seq, hcols:, :] = weigh.astype(BF)

    ga.from_pair()
    for k in range(1, nseq):
        pltpu.make_async_remote_copy(
            src_ref=xa.at[0],
            dst_ref=xa.at[lax.rem(seq + nseq - k, nseq)],
            send_sem=r_send.at[k],
            recv_sem=r_recv.at[k],
            device_id=(lax.rem(seq + k, nseq), tp),
            device_id_type=MESH,
        ).wait_recv()
    xb[tp] = xa[...]
    gx = PairFirst(over_tp, xb, (0, nseq // 2, nseq), x_send, x_recv)
    gx.start()
    ga.from_ring()
    ga.from_far()

    arows = ntp * adapter.shape[0]
    for k in range(ntp):
        ebuf[seq, k * adapter.shape[0] : (k + 1) * adapter.shape[0], :] = abuf[
            k, :, pl.ds(pl.multiple_of(tp * ecols, HD), ecols)
        ]
    ge = RingFirst(over_seq, ebuf, (0, arows // 2, arows), e_send, e_recv)
    ge.start()
    scaled[...] = (abuf[...].reshape(arows, wide).astype(F32) * user_gain[...]).astype(BF)
    for i, load in enumerate(loads):
        load.wait()
        mix[seq, :, i * hcols : (i + 1) * hcols] = dot(scaled[...], weights[i]).astype(BF)
    gm = PairFirst(over_seq, mix, (0, arows // 2, arows), m_send, m_recv)
    gm.start()

    gx.from_pair()
    ge.from_pair()
    gm.from_pair()
    ge.from_ring()
    gx.from_ring()
    gm.from_ring()
    ge.pair_ring()
    gx.from_far()
    for k in range(ntp):
        size = nchosen * chunks
        spread[pl.ds(k * size, size), :] = xb[k].reshape(size, HD).astype(F32)
    for k in range(chunks):
        rows[:, k * HD : (k + 1) * HD] = spread[pl.ds(k, nslot, stride=chunks), :].astype(BF)
    ge.from_far()
    gm.from_far()
    ge.pair_far()
    for gather in (ge, gm):
        gather.sib_own()
        gather.sib_ring()
        gather.sib_far()

    square = jnp.zeros((nslot, HD), F32)
    tile = min(256, ecols)
    for j in range(ecols // tile):
        emb = dot(rows[...], ebuf[:, :, j * tile : (j + 1) * tile].reshape(ditem, tile))
        for i in range(tile // HD):
            piece = emb[:, i * HD : (i + 1) * HD]
            square = square + piece * piece
    sums[tp] = jnp.broadcast_to(jnp.sum(square.T, axis=0, keepdims=True), (8, nslot))
    shared = []
    for k in range(1, ntp):
        copy = pltpu.make_async_remote_copy(
            src_ref=sums.at[tp],
            dst_ref=sums.at[tp],
            send_sem=s_send.at[k],
            recv_sem=s_recv.at[k],
            device_id=(seq, lax.rem(tp + k, ntp)),
            device_id_type=MESH,
        )
        copy.start()
        shared.append(copy)
    for i in range(3):
        raw[i] = dot(rows[...], mix[:, :, i * hcols : (i + 1) * hcols].reshape(ditem, hcols))
    for k in range(1, ntp):
        other = lax.rem(tp + ntp - k, ntp)
        pltpu.make_async_remote_copy(
            src_ref=sums.at[other],
            dst_ref=sums.at[other],
            send_sem=s_send.at[k],
            recv_sem=s_recv.at[k],
            device_id=(seq, lax.rem(tp + k, ntp)),
            device_id_type=MESH,
        ).wait_recv()
    total = sums[0]
    for k in range(1, ntp):
        total = total + sums[k]
    inverse = lax.rsqrt(total[0:1, :] / wide + EPS)
    down = jnp.broadcast_to(inverse, (HD, nslot)).T
    for h in range(heads):
        span = slice(h * HD, (h + 1) * HD)
        kt[seq, span, :] = (raw[1, :, span].T * inverse).astype(BF)
        val[seq, :, span] = (raw[2, :, span] * down).astype(BF)
        query[:, span] = (raw[0, :, span] * (down * (LOG2E / math.sqrt(HD)))).astype(BF)
    gk = PairFirst(over_seq, kt, (0, hcols // 2, kt.shape[1]), k_send, k_recv)
    gv = RingFirst(over_seq, val, (0, nslot // 2, nslot), v_send, v_recv)
    gk.start()
    gv.start()

    qpos[...] = dot(place[...], query[...]).astype(BF)
    vpos[...] = dot(place[...], val[seq]).astype(BF)
    kpos_t[...] = dot(kt[seq, :hcols, :], place_t[...]).astype(BF)
    step = min(256, npos)
    for h in range(heads):
        span = slice(h * HD, (h + 1) * HD)
        for i in range(npos // step):
            here, upto = slice(i * step, (i + 1) * step), (i + 1) * step
            score = dot(qpos[here, span], kpos_t[span, :upto])
            cols = lax.broadcasted_iota(jnp.int32, (step, upto), 1) + first_pos
            allowed = (cols <= col_pos[here]) & (cols >= begin[here])
            score = jnp.where(allowed, score, EMPTY)
            largest = jnp.max(score, axis=1, keepdims=True)
            prob = jnp.exp2(score - largest).astype(BF)
            both = dot(prob, jnp.concatenate([vpos[:upto, span], jnp.ones((upto, HD), BF)], axis=1))
            near[h, here, :] = both[:, :HD] / both[:, HD:]
            near_log[h, here, :] = largest + jnp.log(both[:, HD:]) * LOG2E
    top[...] = jnp.full(top.shape, FLOOR, F32)
    accum[...] = jnp.zeros(accum.shape, F32)

    user_here = user_of(jnp.zeros((16, nslot), jnp.int32) + first_pos)
    which = lax.broadcasted_iota(jnp.int32, (16, nslot), 0)
    chosen_rows = (which % USERS == user_here) & (which < 3 * USERS)
    ones = jnp.ones((nslot, HD), BF)

    def attend(ring):
        def block(i, carry):
            other = ring * 4 + i

            @pl.when(other < seq)
            def _():
                tail = kt[other, hcols:, :].astype(F32)
                bias = jnp.sum(jnp.where(chosen_rows, tail, 0.0), axis=0, keepdims=True)
                for h in range(heads):
                    span = slice(h * HD, (h + 1) * HD)
                    score = dot(query[:, span], kt[other, span, :]) + bias
                    before = top[h]
                    after = jnp.maximum(before, jnp.max(score, axis=1, keepdims=True))
                    prob = jnp.exp2(score - after[:, :1]).astype(BF)
                    shrink = jnp.exp2(before - after)
                    both = dot(prob, jnp.concatenate([val[other, :, span], ones], axis=1))
                    accum[h] = accum[h] * jnp.concatenate([shrink, shrink], axis=1) + both
                    top[h] = after

            return carry

        lax.fori_loop(0, 4, block, 0)

    ring = seq // 4
    gk.from_pair()
    gv.from_pair()
    gk.sib_own()
    gv.sib_own()
    attend(ring)
    gv.from_ring()
    gk.from_ring()
    gv.pair_ring()
    gk.sib_ring()
    gv.sib_ring()
    attend((ring + 3) % 4)
    attend((ring + 1) % 4)
    gv.from_far()
    gk.from_far()
    gv.pair_far()
    gk.sib_far()
    gv.sib_far()
    attend((ring + 2) % 4)

    lane = lax.broadcasted_iota(jnp.int32, (nslot, HD), 1)
    reaches = begin < first_pos
    for h in range(heads):
        span = slice(h * HD, (h + 1) * HD)
        weight = accum[h, :, HD:]
        some = weight > 0.0
        far = accum[h, :, :HD] / jnp.where(some, weight, 1.0)
        far_log = jnp.where(some, top[h] + jnp.log(jnp.where(some, weight, 1.0)) * LOG2E, FLOOR)
        parts = pieces(far_log)
        packed = jnp.where(lane == 0, parts[0], jnp.where(lane == 1, parts[1], jnp.where(lane == 2, parts[2], 0.0)))
        moved = dot(place[...], jnp.concatenate([far.astype(BF), packed.astype(BF)], axis=1))
        far_log = jnp.sum(moved[:, HD:], axis=1, keepdims=True)
        far_log = jnp.where(reaches, far_log, FLOOR)
        near_here = near_log[h]
        both = jnp.maximum(near_here, far_log)
        near_weight = jnp.exp2(near_here - both)
        far_weight = jnp.exp2(far_log - both)
        mean = (near[h] * near_weight + moved[:, :HD] * far_weight) / (near_weight + far_weight)
        out[:, span] = mean.astype(BF)

    for gather in (ga, gx, ge, gm, gk, gv):
        gather.finish()
    for copy in routed + shared:
        copy.wait_send()


def per_device(
    item_states,
    item_gain,
    adapter,
    send_rows,
    hist_slot,
    hist_lengths,
    user_gain,
    w_query,
    w_key,
    w_value,
):
    ntp, nseq = lax.axis_size("tp"), lax.axis_size("seq")
    cap = send_rows.shape[2]
    arows, wide = adapter.shape
    ditem = item_states.shape[1]
    hcols = w_query.shape[1]
    heads = hcols // HD
    npos = hist_slot.shape[0]
    nchosen = nseq * cap
    nslot = ntp * nchosen
    chunks = ditem // HD
    ecols = wide // ntp
    device, column = hist_slot // cap, hist_slot % cap
    slots = ((device % ntp) * nseq + device // ntp) * cap + column
    vmem = pl.BlockSpec(memory_space=pltpu.VMEM)
    hbm = pl.BlockSpec(memory_space=pl.ANY)
    dma = pltpu.SemaphoreType.DMA
    scratch = [
        pltpu.VMEM((ntp, arows, wide), BF),
        pltpu.VMEM((ntp * arows, wide), BF),
        pltpu.VMEM((3, wide, hcols), BF),
        pltpu.VMEM((nslot * chunks, HD), F32),
        pltpu.VMEM((nchosen, chunks, HD), BF),
        pltpu.VMEM((nseq, cap, chunks, HD), BF),
        pltpu.VMEM((ntp, nseq, cap, chunks, HD), BF),
        pltpu.VMEM((nslot, ditem), BF),
        pltpu.VMEM((nseq, ntp * arows, 3 * hcols), BF),
        pltpu.VMEM((nseq, ntp * arows, ecols), BF),
        pltpu.VMEM((3, nslot, hcols), F32),
        pltpu.VMEM((ntp, 8, nslot), F32),
        pltpu.VMEM((nslot, hcols), BF),
        pltpu.VMEM((nseq, hcols + 16, nslot), BF),
        pltpu.VMEM((nseq, nslot, hcols), BF),
        pltpu.VMEM((npos, nslot), BF),
        pltpu.VMEM((nslot, npos), BF),
        pltpu.VMEM((npos, hcols), BF),
        pltpu.VMEM((hcols, npos), BF),
        pltpu.VMEM((npos, hcols), BF),
        pltpu.VMEM((heads, npos, HD), F32),
        pltpu.VMEM((heads, npos, HD), F32),
        pltpu.VMEM((heads, nslot, HD), F32),
        pltpu.VMEM((heads, nslot, 2 * HD), F32),
        dma((3,)),
        dma((9,)),
        dma((9,)),
        dma((nseq,)),
        dma((nseq,)),
        dma((9,)),
        dma((9,)),
        dma((17,)),
        dma((17,)),
        dma((16,)),
        dma((16,)),
        dma((ntp,)),
        dma((ntp,)),
        dma((17,)),
        dma((17,)),
        dma((16,)),
        dma((16,)),
    ]
    return pl.pallas_call(
        kernel,
        out_shape=jax.ShapeDtypeStruct((npos, hcols), BF),
        in_specs=[pl.BlockSpec(memory_space=pltpu.SMEM)] + [vmem] * 7 + [hbm] * 3,
        out_specs=vmem,
        scratch_shapes=scratch,
        compiler_params=pltpu.CompilerParams(
            collective_id=0, has_side_effects=True, vmem_limit_bytes=56 * 1024 * 1024
        ),
    )(
        hist_lengths,
        item_states,
        item_gain.reshape(1, -1),
        adapter,
        send_rows[:, 0, :].reshape(-1, 1),
        slots.reshape(1, -1),
        slots.reshape(-1, 1),
        user_gain.reshape(1, -1),
        w_query,
        w_key,
        w_value,
    )


def solution(mesh):
    in_specs = (
        P(("seq", "tp"), None),
        P(),
        P(("seq", "tp"), None),
        P(None, ("seq", "tp"), None),
        P("seq"),
        P(),
        P(),
        P(None, "tp"),
        P(None, "tp"),
        P(None, "tp"),
    )
    return jax.shard_map(
        per_device, mesh=mesh, in_specs=in_specs, out_specs=P("seq", "tp"), check_vma=False
    )
```

time: 763 us -> 127 us (0.17)
  the two profiles are of different devices: /device:TPU:6 before, /device:TPU:15 now
where the time goes in v1:
time: 127 us
  Pallas kernels  122 us (96%)
  local copies, waits for them, and re-layouts  4.34 us (3%)
    pallas_call x1, Pallas kernels, per_device(): pl.pallas_call(kernel, out_shape=jax.ShapeDtypeStruct((npos, hcols), BF),...  122 us
    unnamed x4, local copies, waits for them, and re-layouts  2.63 us

profile of v1, /device:TPU:15, one launch (start us, length us, event | category | flops | bytes accessed | tf_op | source)
XLA Modules:
  0.0 126.6 jit_solution(10820201680355496840)
XLA Ops:
  0.0 0.7 fusion.3
  0.7 0.0 copy-start
  0.7 0.8 copy.13
  1.5 0.7 reshape_squeeze.4.picks
  2.2 1.0 copy.15.slot_col
  3.2 0.0 copy-done
  3.2 121.5 %shard_map.100 = bf16[1024,256]{1,0:T(8,128)(2,1)} custom-call(s32[4]{0:T(128)} %lengths.1, bf16[256,2048]{1,0:T(8,128)(2,1)} %items.1, f32[1,2048]{1,0:T(1,128)} %bitcast.9, bf16[16,4096]{1,0:T(8,128)(2,1)} %adapter.1, s32[64,1]{1,0:T(8,128)} %reshape_squeeze.4.picks, s32[1,1024]{1,0:T(1,128)} %bitcast.7, s32[1024,1]{1,0:T(8,128)} %copy.15.slot_col, ...), custom_call_target="tpu_custom_call" | custom-call | tf_op jit(solution)/shard_map/pallas_call | solution.py:617
  124.7 1.9 %copy.17 = bf16[1024,256]{1,0:T(8,128)(2,1)} copy(bf16[1024,256]{1,0:T(8,128)(2,1)} %shard_map.100) | data formatting | bytes 1048576
Async XLA Ops:
  0.7 2.5 %copy-start = (s32[1024]{0:T(1024)}, s32[1024]{0:T(1024)S(1)}, u32[]{:S(2)}) copy-start(s32[1024]{0:T(1024)S(1)} %fusion.3) | copy-start | bytes 12292

commit v2 on v1

--- a/solution.py
+++ b/solution.py
@@ -220,8 +220,7 @@
     item_gain,
     adapter,
     picks,
-    slot_row,
-    slot_col,
+    slots,
     user_gain,
     w_query,
     w_key,
@@ -256,6 +255,8 @@
     a_recv,
     r_send,
     r_recv,
+    c_send,
+    c_recv,
     x_send,
     x_recv,
     m_send,
@@ -296,7 +297,11 @@
         peer = (lax.rem(seq + k, nseq), tp)
         pl.semaphore_signal(barrier, inc=1, device_id=peer, device_id_type=MESH)
 
-    pick = (lax.broadcasted_iota(jnp.int32, (nchosen, items.shape[0]), 1) == picks[...]).astype(BF)
+    which = lax.broadcasted_iota(jnp.int32, (nchosen, 1), 0)
+    column = jnp.zeros((nchosen, 1), jnp.int32)
+    for r in range(nchosen):
+        column = jnp.where(which == r, picks[r % cap, r // cap], column)
+    pick = (lax.broadcasted_iota(jnp.int32, (nchosen, items.shape[0]), 1) == column).astype(BF)
     chosen = dot(pick, items[...])
     factor = lax.rsqrt(jnp.mean(chosen * chosen, axis=1, keepdims=True) + EPS)
     chosen = chosen * factor * item_gain[...]
@@ -307,24 +312,67 @@
     pl.semaphore_wait(barrier, ntp + nseq - 2)
 
     over_tp, over_seq = Group("tp"), Group("seq")
+    arows = adapter.shape[0]
 
     abuf[tp] = adapter[...]
     ga = PairFirst(over_tp, abuf, (1, wide // 2, wide), a_send, a_recv)
     ga.start()
-    routed = []
-    for k in range(1, nseq):
-        peer = lax.rem(seq + k, nseq)
-        copy = pltpu.make_async_remote_copy(
+
+    def columns_of(index):
+        return adapter.at[:, pl.ds(pl.multiple_of(index * ecols, HD), ecols)]
+
+    def column_copy(k, peer, source):
+        return pltpu.make_async_remote_copy(
+            src_ref=columns_of(peer),
+            dst_ref=ebuf.at[seq, pl.ds(pl.multiple_of(source * arows, arows), arows)],
+            send_sem=c_send.at[k],
+            recv_sem=c_recv.at[k],
+            device_id=(seq, peer),
+            device_id_type=MESH,
+        )
+
+    def routed_copy(k, peer, source):
+        return pltpu.make_async_remote_copy(
             src_ref=xs.at[pl.ds(peer * cap, cap)],
-            dst_ref=xa.at[seq],
+            dst_ref=xa.at[source],
             send_sem=r_send.at[k],
             recv_sem=r_recv.at[k],
             device_id=(peer, tp),
             device_id_type=MESH,
         )
-        copy.start()
-        routed.append(copy)
+
+    straight = []
+    for k in range(1, ntp):
+        straight.append(column_copy(k, lax.rem(tp + k, ntp), tp))
+        straight[-1].start()
+    for k in range(1, nseq):
+        straight.append(routed_copy(k, lax.rem(seq + k, nseq), seq))
+        straight[-1].start()
     xa[seq] = xs[pl.ds(seq * cap, cap)]
+    ebuf[seq, pl.ds(pl.multiple_of(tp * arows, arows), arows), :] = adapter[
+        :, pl.ds(pl.multiple_of(tp * ecols, HD), ecols)
+    ]
+
+    origin = slots[...] // cap
+    spot = ((origin % ntp) * nseq + origin // ntp) * cap + slots[...] % cap
+    groups = spot.shape[0]
+    spot_t = jnp.concatenate([spot.astype(F32), jnp.zeros((HD - groups, HD), F32)], axis=0).T.astype(jnp.int32)
+    for k in range(groups):
+        here = slice(k * HD, (k + 1) * HD)
+        place_t[:, here] = (lax.broadcasted_iota(jnp.int32, (nslot, HD), 0) == spot[k : k + 1, :]).astype(BF)
+        place[here, :] = (lax.broadcasted_iota(jnp.int32, (HD, nslot), 1) == spot_t[:, k : k + 1]).astype(BF)
+
+    ga.from_pair()
+    for k in range(1, ntp):
+        column_copy(k, lax.rem(tp + k, ntp), lax.rem(tp + ntp - k, ntp)).wait_recv()
+    ge = RingFirst(over_seq, ebuf, (0, ntp * arows // 2, ntp * arows), e_send, e_recv)
+    ge.start()
+    ga.from_ring()
+    for k in range(1, nseq):
+        routed_copy(k, lax.rem(seq + k, nseq), lax.rem(seq + nseq - k, nseq)).wait_recv()
+    xb[tp] = xa[...]
+    gx = PairFirst(over_tp, xb, (0, nseq // 2, nseq), x_send, x_recv)
+    gx.start()
 
     ends = [lengths[0]]
     for u in range(1, USERS):
@@ -341,8 +389,6 @@
     begin = jnp.zeros_like(col_pos)
     for end in ends:
         begin = jnp.maximum(begin, jnp.where(col_pos >= end, end, 0))
-    place[...] = (lax.broadcasted_iota(jnp.int32, (npos, nslot), 1) == slot_col[...]).astype(BF)
-    place_t[...] = (lax.broadcasted_iota(jnp.int32, (nslot, npos), 0) == slot_row[...]).astype(BF)
     belongs = lax.broadcasted_iota(jnp.int32, (16, npos), 0) % USERS == user_of(row_pos)
     held = dot(belongs.astype(BF), place[...])
     weigh = jnp.where(held > 0.5, jnp.log(jnp.maximum(held, 1.0)) * LOG2E, EMPTY)
@@ -351,29 +397,8 @@
     weigh = jnp.where(part == 0, parts[0], jnp.where(part == 1, parts[1], jnp.where(part == 2, parts[2], 0.0)))
     kt[seq, hcols:, :] = weigh.astype(BF)
 
-    ga.from_pair()
-    for k in range(1, nseq):
-        pltpu.make_async_remote_copy(
-            src_ref=xa.at[0],
-            dst_ref=xa.at[lax.rem(seq + nseq - k, nseq)],
-            send_sem=r_send.at[k],
-            recv_sem=r_recv.at[k],
-            device_id=(lax.rem(seq + k, nseq), tp),
-            device_id_type=MESH,
-        ).wait_recv()
-    xb[tp] = xa[...]
-    gx = PairFirst(over_tp, xb, (0, nseq // 2, nseq), x_send, x_recv)
-    gx.start()
-    ga.from_ring()
     ga.from_far()
-
-    arows = ntp * adapter.shape[0]
-    for k in range(ntp):
-        ebuf[seq, k * adapter.shape[0] : (k + 1) * adapter.shape[0], :] = abuf[
-            k, :, pl.ds(pl.multiple_of(tp * ecols, HD), ecols)
-        ]
-    ge = RingFirst(over_seq, ebuf, (0, arows // 2, arows), e_send, e_recv)
-    ge.start()
+    arows = ntp * arows
     scaled[...] = (abuf[...].reshape(arows, wide).astype(F32) * user_gain[...]).astype(BF)
     for i, load in enumerate(loads):
         load.wait()
@@ -381,26 +406,24 @@
     gm = PairFirst(over_seq, mix, (0, arows // 2, arows), m_send, m_recv)
     gm.start()
 
+    ge.from_pair()
+    ge.from_ring()
     gx.from_pair()
-    ge.from_pair()
+    ge.pair_ring()
     gm.from_pair()
-    ge.from_ring()
+    ge.from_far()
     gx.from_ring()
     gm.from_ring()
-    ge.pair_ring()
+    ge.pair_far()
     gx.from_far()
     for k in range(ntp):
         size = nchosen * chunks
         spread[pl.ds(k * size, size), :] = xb[k].reshape(size, HD).astype(F32)
     for k in range(chunks):
         rows[:, k * HD : (k + 1) * HD] = spread[pl.ds(k, nslot, stride=chunks), :].astype(BF)
-    ge.from_far()
-    gm.from_far()
-    ge.pair_far()
-    for gather in (ge, gm):
-        gather.sib_own()
-        gather.sib_ring()
-        gather.sib_far()
+    ge.sib_own()
+    ge.sib_ring()
+    ge.sib_far()
 
     square = jnp.zeros((nslot, HD), F32)
     tile = min(256, ecols)
@@ -422,6 +445,10 @@
         )
         copy.start()
         shared.append(copy)
+    gm.from_far()
+    gm.sib_own()
+    gm.sib_ring()
+    gm.sib_far()
     for i in range(3):
         raw[i] = dot(rows[...], mix[:, :, i * hcols : (i + 1) * hcols].reshape(ditem, hcols))
     for k in range(1, ntp):
@@ -473,49 +500,58 @@
     which = lax.broadcasted_iota(jnp.int32, (16, nslot), 0)
     chosen_rows = (which % USERS == user_here) & (which < 3 * USERS)
     ones = jnp.ones((nslot, HD), BF)
+    band = min(128, nslot)
 
     def attend(ring):
-        def block(i, carry):
-            other = ring * 4 + i
-
-            @pl.when(other < seq)
-            def _():
-                tail = kt[other, hcols:, :].astype(F32)
-                bias = jnp.sum(jnp.where(chosen_rows, tail, 0.0), axis=0, keepdims=True)
-                for h in range(heads):
-                    span = slice(h * HD, (h + 1) * HD)
-                    score = dot(query[:, span], kt[other, span, :]) + bias
-                    before = top[h]
-                    after = jnp.maximum(before, jnp.max(score, axis=1, keepdims=True))
-                    prob = jnp.exp2(score - after[:, :1]).astype(BF)
-                    shrink = jnp.exp2(before - after)
-                    both = dot(prob, jnp.concatenate([val[other, :, span], ones], axis=1))
-                    accum[h] = accum[h] * jnp.concatenate([shrink, shrink], axis=1) + both
-                    top[h] = after
-
-            return carry
-
-        lax.fori_loop(0, 4, block, 0)
+        bias = []
+        for i in range(4):
+            tail = kt[ring * 4 + i, hcols:, :].astype(F32)
+            line = jnp.sum(jnp.where(chosen_rows, tail, 0.0), axis=0, keepdims=True)
+            bias.append(jnp.where(jnp.zeros_like(line, jnp.int32) + ring * 4 + i < seq, line, EMPTY))
+        for h in range(heads):
+            span = slice(h * HD, (h + 1) * HD)
+            for b in range(nslot // band):
+                here = slice(b * band, (b + 1) * band)
+                asked = query[here, span]
+                scores = [dot(asked, kt[ring * 4 + i, span, :]) + bias[i] for i in range(4)]
+                largest = jnp.maximum(jnp.maximum(scores[0], scores[1]), jnp.maximum(scores[2], scores[3]))
+                before = top[h, here]
+                after = jnp.maximum(before, jnp.max(largest, axis=1, keepdims=True))
+                both = None
+                for i in range(4):
+                    prob = jnp.exp2(scores[i] - after[:, :1]).astype(BF)
+                    part = dot(prob, jnp.concatenate([val[ring * 4 + i, :, span], ones], axis=1))
+                    both = part if both is None else both + part
+                shrink = jnp.exp2(before - after)
+                accum[h, here] = accum[h, here] * jnp.concatenate([shrink, shrink], axis=1) + both
+                top[h, here] = after
+
+    def attend_earlier(step):
+        other = (ring + step) % 4
+
+        @pl.when(other < ring)
+        def _():
+            attend(other)
 
     ring = seq // 4
     gk.from_pair()
+    gv.from_ring()
     gv.from_pair()
     gk.sib_own()
     gv.sib_own()
     attend(ring)
-    gv.from_ring()
     gk.from_ring()
+    gv.from_far()
     gv.pair_ring()
     gk.sib_ring()
     gv.sib_ring()
-    attend((ring + 3) % 4)
-    attend((ring + 1) % 4)
-    gv.from_far()
+    attend_earlier(3)
+    attend_earlier(1)
     gk.from_far()
     gv.pair_far()
     gk.sib_far()
     gv.sib_far()
-    attend((ring + 2) % 4)
+    attend_earlier(2)
 
     lane = lax.broadcasted_iota(jnp.int32, (nslot, HD), 1)
     reaches = begin < first_pos
@@ -539,7 +575,7 @@
 
     for gather in (ga, gx, ge, gm, gk, gv):
         gather.finish()
-    for copy in routed + shared:
+    for copy in straight + shared:
         copy.wait_send()
 
 
@@ -566,9 +602,8 @@
     nslot = ntp * nchosen
     chunks = ditem // HD
     ecols = wide // ntp
-    device, column = hist_slot // cap, hist_slot % cap
-    slots = ((device % ntp) * nseq + device // ntp) * cap + column
     vmem = pl.BlockSpec(memory_space=pltpu.VMEM)
+    smem = pl.BlockSpec(memory_space=pltpu.SMEM)
     hbm = pl.BlockSpec(memory_space=pl.ANY)
     dma = pltpu.SemaphoreType.DMA
     scratch = [
@@ -601,6 +636,8 @@
         dma((9,)),
         dma((nseq,)),
         dma((nseq,)),
+        dma((ntp,)),
+        dma((ntp,)),
         dma((9,)),
         dma((9,)),
         dma((17,)),
@@ -617,7 +654,7 @@
     return pl.pallas_call(
         kernel,
         out_shape=jax.ShapeDtypeStruct((npos, hcols), BF),
-        in_specs=[pl.BlockSpec(memory_space=pltpu.SMEM)] + [vmem] * 7 + [hbm] * 3,
+        in_specs=[smem, vmem, vmem, vmem, smem, vmem, vmem] + [hbm] * 3,
         out_specs=vmem,
         scratch_shapes=scratch,
         compiler_params=pltpu.CompilerParams(
@@ -628,9 +665,8 @@
         item_states,
         item_gain.reshape(1, -1),
         adapter,
-        send_rows[:, 0, :].reshape(-1, 1),
-        slots.reshape(1, -1),
-        slots.reshape(-1, 1),
+        send_rows.transpose(1, 2, 0).reshape(cap, nseq),
+        hist_slot.reshape(-1, HD),
         user_gain.reshape(1, -1),
         w_query,
         w_key,

time: 127 us -> 99.4 us (0.78)
  the two profiles are of different devices: /device:TPU:15 before, /device:TPU:6 now
where the time goes in v2:
time: 99.4 us; the launch traced here: 99.2 us
  Pallas kernels  97.3 us (98%)
  local copies, waits for them, and re-layouts  1.87 us (2%)
    pallas_call x1, Pallas kernels, per_device(): pl.pallas_call(kernel, out_shape=jax.ShapeDtypeStruct((npos, hcols), BF),...  97.3 us

profile of v2, /device:TPU:6, one launch (start us, length us, event | category | flops | bytes accessed | tf_op | source)
XLA Modules:
  0.0 99.2 jit_solution(990780227097400299)
XLA Ops:
  0.0 97.3 %shard_map.100 = bf16[1024,256]{1,0:T(8,128)(2,1)} custom-call(s32[4]{0:T(128)} %lengths.1, bf16[256,2048]{1,0:T(8,128)(2,1)} %items.1, f32[1,2048]{1,0:T(1,128)} %bitcast.7, bf16[16,4096]{1,0:T(8,128)(2,1)} %adapter.1, s32[4,16]{1,0:T(4,128)} %bitcast.9, s32[8,128]{1,0:T(8,128)} %bitcast.8, f32[1,4096]{1,0:T(1,128)} %bitcast.6, bf16[4096,256]{1,0:T(8,128)(2,1)} %w_query.1, ...), custom_call_target="tpu_custom_call" | custom-call | tf_op jit(solution)/shard_map/pallas_call | solution.py:654
  97.3 1.9 %copy.12 = bf16[1024,256]{1,0:T(8,128)(2,1)} copy(bf16[1024,256]{1,0:T(8,128)(2,1)} %shard_map.100) | data formatting | bytes 1048576

commit v3 on v2

--- a/solution.py
+++ b/solution.py
@@ -54,10 +54,10 @@
         piece = pl.ds(0, cut) if part == 0 else pl.ds(cut, end - cut)
         return ref.at[(slice(None),) * axis + (piece,)]
 
-    def push(self, index, device, slot, part=None):
+    def push(self, index, device, slot, part=None, source=None):
         ref = self.view(index, part)
         copy = pltpu.make_async_remote_copy(
-            src_ref=ref,
+            src_ref=ref if source is None else source,
             dst_ref=ref,
             send_sem=self.send.at[self.count],
             recv_sem=self.recv.at[slot],
@@ -85,10 +85,10 @@
 
 
 class PairFirst(Gather):
-    def start(self):
+    def start(self, for_pair=None):
         g = self.g
         own = g.block()
-        self.push(own, g.pair, 0)
+        self.push(own, g.pair, 0, source=for_pair)
         self.push(own, g.right, 1)
         self.push(own, g.left, 3)
         if g.cores:
@@ -138,74 +138,6 @@
     def sib_far(self):
         for dp in (0, 1):
             self.got(self.g.block(2, dp, 1), 15 + dp)
-
-
-class RingFirst(Gather):
-    def start(self):
-        g = self.g
-        own = g.block()
-        self.push(own, g.right, 1)
-        self.push(own, g.left, 2)
-        self.push(own, g.pair, 0)
-        self.push(own, g.sib, 8)
-
-    def from_pair(self):
-        block = self.g.block(0, 1)
-        self.got(block, 0)
-        self.push(block, self.g.sib, 9)
-
-    def from_ring(self):
-        g = self.g
-        block = g.block(3, 0)
-        self.got(block, 1)
-        self.push(block, g.right, 3, 0)
-        self.push(block, g.pair, 5)
-        self.push(block, g.sib, 10)
-        block = g.block(1, 0)
-        self.got(block, 2)
-        self.push(block, g.left, 4, 1)
-        self.push(block, g.pair, 6)
-        self.push(block, g.sib, 11)
-
-    def from_far(self):
-        g = self.g
-        block = g.block(2, 0)
-        self.got(block, 3, 0)
-        self.got(block, 4, 1)
-        self.push(block, g.pair, 7)
-        self.push(block, g.sib, 12)
-
-    def pair_ring(self):
-        g = self.g
-        block = g.block(3, 1)
-        self.got(block, 5)
-        self.push(block, g.sib, 13)
-        block = g.block(1, 1)
-        self.got(block, 6)
-        self.push(block, g.sib, 14)
-
-    def pair_far(self):
-        g = self.g
-        block = g.block(2, 1)
-        self.got(block, 7)
-        self.push(block, g.sib, 15)
-
-    def sib_own(self):
-        g = self.g
-        self.got(g.block(0, 0, 1), 8)
-        self.got(g.block(0, 1, 1), 9)
-
-    def sib_ring(self):
-        g = self.g
-        self.got(g.block(3, 0, 1), 10)
-        self.got(g.block(1, 0, 1), 11)
-        self.got(g.block(3, 1, 1), 13)
-        self.got(g.block(1, 1, 1), 14)
-
-    def sib_far(self):
-        g = self.g
-        self.got(g.block(2, 0, 1), 12)
-        self.got(g.block(2, 1, 1), 15)
 
 
 def pieces(values):
@@ -239,8 +171,13 @@
     raw,
     sums,
     query,
+    kown,
+    vown,
+    asked,
     kt,
     val,
+    means,
+    logs,
     place,
     place_t,
     qpos,
@@ -269,6 +206,8 @@
     k_recv,
     v_send,
     v_recv,
+    p_send,
+    p_recv,
 ):
     seq, tp = lax.axis_index("seq"), lax.axis_index("tp")
     nseq, ntp = lax.axis_size("seq"), lax.axis_size("tp")
@@ -307,7 +246,7 @@
     chosen = chosen * factor * item_gain[...]
     for k in range(chunks):
         spread[pl.ds(k, nchosen, stride=chunks), :] = chosen[:, k * HD : (k + 1) * HD]
-    xs[...] = spread[: nchosen * chunks].reshape(nchosen, chunks, HD).astype(BF)
+    xs[...] = spread[...].reshape(nchosen, chunks, HD).astype(BF)
 
     pl.semaphore_wait(barrier, ntp + nseq - 2)
 
@@ -365,14 +304,23 @@
     ga.from_pair()
     for k in range(1, ntp):
         column_copy(k, lax.rem(tp + k, ntp), lax.rem(tp + ntp - k, ntp)).wait_recv()
-    ge = RingFirst(over_seq, ebuf, (0, ntp * arows // 2, ntp * arows), e_send, e_recv)
+    ge = PairFirst(over_seq, ebuf, (0, ntp * arows // 2, ntp * arows), e_send, e_recv)
     ge.start()
-    ga.from_ring()
     for k in range(1, nseq):
         routed_copy(k, lax.rem(seq + k, nseq), lax.rem(seq + nseq - k, nseq)).wait_recv()
     xb[tp] = xa[...]
     gx = PairFirst(over_tp, xb, (0, nseq // 2, nseq), x_send, x_recv)
     gx.start()
+    ga.from_ring()
+    ge.from_pair()
+
+    def lay_out(block):
+        size = nchosen * chunks
+        spread[...] = xb[block].reshape(size, HD).astype(F32)
+        first = pl.multiple_of(block * nchosen, nchosen)
+        for k in range(chunks):
+            piece = spread[pl.ds(k, nchosen, stride=chunks), :]
+            rows[pl.ds(first, nchosen), k * HD : (k + 1) * HD] = piece.astype(BF)
 
     ends = [lengths[0]]
     for u in range(1, USERS):
@@ -395,7 +343,8 @@
     parts = pieces(weigh)
     part = lax.broadcasted_iota(jnp.int32, (16, nslot), 0) // USERS
     weigh = jnp.where(part == 0, parts[0], jnp.where(part == 1, parts[1], jnp.where(part == 2, parts[2], 0.0)))
-    kt[seq, hcols:, :] = weigh.astype(BF)
+    for h in range(heads):
+        kown[h, HD:, :] = weigh.astype(BF)
 
     ga.from_far()
     arows = ntp * arows
@@ -406,21 +355,20 @@
     gm = PairFirst(over_seq, mix, (0, arows // 2, arows), m_send, m_recv)
     gm.start()
 
-    ge.from_pair()
+    gx.from_pair()
     ge.from_ring()
-    gx.from_pair()
-    ge.pair_ring()
+    lay_out(over_tp.block())
+    lay_out(over_tp.block(0, 1))
     gm.from_pair()
     ge.from_far()
     gx.from_ring()
+    for dp in (0, 1):
+        lay_out(over_tp.block(3, dp))
+        lay_out(over_tp.block(1, dp))
     gm.from_ring()
-    ge.pair_far()
     gx.from_far()
-    for k in range(ntp):
-        size = nchosen * chunks
-        spread[pl.ds(k * size, size), :] = xb[k].reshape(size, HD).astype(F32)
-    for k in range(chunks):
-        rows[:, k * HD : (k + 1) * HD] = spread[pl.ds(k, nslot, stride=chunks), :].astype(BF)
+    for dp in (0, 1):
+        lay_out(over_tp.block(2, dp))
     ge.sib_own()
     ge.sib_ring()
     ge.sib_far()
@@ -466,116 +414,151 @@
         total = total + sums[k]
     inverse = lax.rsqrt(total[0:1, :] / wide + EPS)
     down = jnp.broadcast_to(inverse, (HD, nslot)).T
+    mine = (seq // 2) % 2
+    theirs = 1 - mine
     for h in range(heads):
-        span = slice(h * HD, (h + 1) * HD)
-        kt[seq, span, :] = (raw[1, :, span].T * inverse).astype(BF)
-        val[seq, :, span] = (raw[2, :, span] * down).astype(BF)
-        query[:, span] = (raw[0, :, span] * (down * (LOG2E / math.sqrt(HD)))).astype(BF)
-    gk = PairFirst(over_seq, kt, (0, hcols // 2, kt.shape[1]), k_send, k_recv)
-    gv = RingFirst(over_seq, val, (0, nslot // 2, nslot), v_send, v_recv)
-    gk.start()
-    gv.start()
-
-    qpos[...] = dot(place[...], query[...]).astype(BF)
-    vpos[...] = dot(place[...], val[seq]).astype(BF)
-    kpos_t[...] = dot(kt[seq, :hcols, :], place_t[...]).astype(BF)
+        kown[h, :HD, :] = (raw[1, :, h * HD : (h + 1) * HD].T * inverse).astype(BF)
+    kt[seq] = kown[mine]
+    gk = PairFirst(over_seq, kt, (0, 64, kt.shape[1]), k_send, k_recv)
+    gk.start(kown.at[theirs])
+    for h in range(heads):
+        vown[h] = (raw[2, :, h * HD : (h + 1) * HD] * down).astype(BF)
+    val[seq] = vown[mine]
+    gv = PairFirst(over_seq, val, (0, nslot // 2, nslot), v_send, v_recv)
+    gv.start(vown.at[theirs])
+    for h in range(heads):
+        query[h] = (raw[0, :, h * HD : (h + 1) * HD] * (down * (LOG2E / math.sqrt(HD)))).astype(BF)
+
+    def to_pair(k, source, target):
+        return pltpu.make_async_remote_copy(
+            src_ref=source,
+            dst_ref=target,
+            send_sem=p_send.at[k],
+            recv_sem=p_recv.at[k],
+            device_id=over_seq.pair,
+            device_id_type=MESH,
+        )
+
+    asking = to_pair(0, query.at[theirs], asked.at[1])
+    asking.start()
+    asked[0] = query[mine]
+
     step = min(256, npos)
-    for h in range(heads):
-        span = slice(h * HD, (h + 1) * HD)
+
+    def attend_near(h):
+        qpos[...] = dot(place[...], query[h]).astype(BF)
+        vpos[...] = dot(place[...], vown[h]).astype(BF)
+        kpos_t[...] = dot(kown[h, :HD, :], place_t[...]).astype(BF)
         for i in range(npos // step):
             here, upto = slice(i * step, (i + 1) * step), (i + 1) * step
-            score = dot(qpos[here, span], kpos_t[span, :upto])
+            score = dot(qpos[here], kpos_t[:, :upto])
             cols = lax.broadcasted_iota(jnp.int32, (step, upto), 1) + first_pos
             allowed = (cols <= col_pos[here]) & (cols >= begin[here])
             score = jnp.where(allowed, score, EMPTY)
             largest = jnp.max(score, axis=1, keepdims=True)
             prob = jnp.exp2(score - largest).astype(BF)
-            both = dot(prob, jnp.concatenate([vpos[:upto, span], jnp.ones((upto, HD), BF)], axis=1))
+            both = dot(prob, jnp.concatenate([vpos[:upto], jnp.ones((upto, HD), BF)], axis=1))
             near[h, here, :] = both[:, :HD] / both[:, HD:]
             near_log[h, here, :] = largest + jnp.log(both[:, HD:]) * LOG2E
+
     top[...] = jnp.full(top.shape, FLOOR, F32)
     accum[...] = jnp.zeros(accum.shape, F32)
 
-    user_here = user_of(jnp.zeros((16, nslot), jnp.int32) + first_pos)
     which = lax.broadcasted_iota(jnp.int32, (16, nslot), 0)
-    chosen_rows = (which % USERS == user_here) & (which < 3 * USERS)
     ones = jnp.ones((nslot, HD), BF)
     band = min(128, nslot)
-
-    def attend(ring):
+    sides = (over_seq.block(), over_seq.block(0, 1))
+
+    def attend(ring, j):
+        user_here = user_of(jnp.zeros((16, nslot), jnp.int32) + sides[j] * npos)
+        chosen_rows = (which % USERS == user_here) & (which < 3 * USERS)
         bias = []
         for i in range(4):
-            tail = kt[ring * 4 + i, hcols:, :].astype(F32)
+            tail = kt[ring * 4 + i, HD:, :].astype(F32)
             line = jnp.sum(jnp.where(chosen_rows, tail, 0.0), axis=0, keepdims=True)
-            bias.append(jnp.where(jnp.zeros_like(line, jnp.int32) + ring * 4 + i < seq, line, EMPTY))
-        for h in range(heads):
-            span = slice(h * HD, (h + 1) * HD)
-            for b in range(nslot // band):
-                here = slice(b * band, (b + 1) * band)
-                asked = query[here, span]
-                scores = [dot(asked, kt[ring * 4 + i, span, :]) + bias[i] for i in range(4)]
-                largest = jnp.maximum(jnp.maximum(scores[0], scores[1]), jnp.maximum(scores[2], scores[3]))
-                before = top[h, here]
-                after = jnp.maximum(before, jnp.max(largest, axis=1, keepdims=True))
-                both = None
-                for i in range(4):
-                    prob = jnp.exp2(scores[i] - after[:, :1]).astype(BF)
-                    part = dot(prob, jnp.concatenate([val[ring * 4 + i, :, span], ones], axis=1))
-                    both = part if both is None else both + part
-                shrink = jnp.exp2(before - after)
-                accum[h, here] = accum[h, here] * jnp.concatenate([shrink, shrink], axis=1) + both
-                top[h, here] = after
-
-    def attend_earlier(step):
+            bias.append(jnp.where(jnp.zeros_like(line, jnp.int32) + ring * 4 + i < sides[j], line, EMPTY))
+        for b in range(nslot // band):
+            here = slice(b * band, (b + 1) * band)
+            scores = [dot(asked[j, here], kt[ring * 4 + i, :HD, :]) + bias[i] for i in range(4)]
+            largest = jnp.maximum(jnp.maximum(scores[0], scores[1]), jnp.maximum(scores[2], scores[3]))
+            before = top[j, here]
+            after = jnp.maximum(before, jnp.max(largest, axis=1, keepdims=True))
+            both = None
+            for i in range(4):
+                prob = jnp.exp2(scores[i] - after[:, :1]).astype(BF)
+                part = dot(prob, jnp.concatenate([val[ring * 4 + i], ones], axis=1))
+                both = part if both is None else both + part
+            shrink = jnp.exp2(before - after)
+            accum[j, here] = accum[j, here] * jnp.concatenate([shrink, shrink], axis=1) + both
+            top[j, here] = after
+
+    def attend_earlier(step, *js):
         other = (ring + step) % 4
 
         @pl.when(other < ring)
         def _():
-            attend(other)
-
-    ring = seq // 4
-    gk.from_pair()
-    gv.from_ring()
-    gv.from_pair()
-    gk.sib_own()
-    gv.sib_own()
-    attend(ring)
-    gk.from_ring()
-    gv.from_far()
-    gv.pair_ring()
-    gk.sib_ring()
-    gv.sib_ring()
-    attend_earlier(3)
-    attend_earlier(1)
-    gk.from_far()
-    gv.pair_far()
-    gk.sib_far()
-    gv.sib_far()
-    attend_earlier(2)
+            for j in js:
+                attend(other, j)
+
+    def far_part(j):
+        weight = accum[j, :, HD:]
+        some = weight > 0.0
+        mean = accum[j, :, :HD] / jnp.where(some, weight, 1.0)
+        log = jnp.where(some, top[j] + jnp.log(jnp.where(some, weight, 1.0)) * LOG2E, FLOOR)
+        return mean.astype(BF), log
 
     lane = lax.broadcasted_iota(jnp.int32, (nslot, HD), 1)
     reaches = begin < first_pos
-    for h in range(heads):
-        span = slice(h * HD, (h + 1) * HD)
-        weight = accum[h, :, HD:]
-        some = weight > 0.0
-        far = accum[h, :, :HD] / jnp.where(some, weight, 1.0)
-        far_log = jnp.where(some, top[h] + jnp.log(jnp.where(some, weight, 1.0)) * LOG2E, FLOOR)
-        parts = pieces(far_log)
+
+    def finish(h, mean, log):
+        parts = pieces(log)
         packed = jnp.where(lane == 0, parts[0], jnp.where(lane == 1, parts[1], jnp.where(lane == 2, parts[2], 0.0)))
-        moved = dot(place[...], jnp.concatenate([far.astype(BF), packed.astype(BF)], axis=1))
+        moved = dot(place[...], jnp.concatenate([mean, packed.astype(BF)], axis=1))
         far_log = jnp.sum(moved[:, HD:], axis=1, keepdims=True)
         far_log = jnp.where(reaches, far_log, FLOOR)
         near_here = near_log[h]
-        both = jnp.maximum(near_here, far_log)
-        near_weight = jnp.exp2(near_here - both)
-        far_weight = jnp.exp2(far_log - both)
-        mean = (near[h] * near_weight + moved[:, :HD] * far_weight) / (near_weight + far_weight)
-        out[:, span] = mean.astype(BF)
+        most = jnp.maximum(near_here, far_log)
+        near_weight = jnp.exp2(near_here - most)
+        far_weight = jnp.exp2(far_log - most)
+        result = (near[h] * near_weight + moved[:, :HD] * far_weight) / (near_weight + far_weight)
+        out[:, pl.ds(pl.multiple_of(h * HD, HD), HD)] = result.astype(BF)
+
+    ring = seq // 4
+    attend_near(0)
+    gk.from_pair()
+    gv.from_pair()
+    attend_near(1)
+    asking.wait_recv()
+    gk.sib_own()
+    gv.sib_own()
+    attend(ring, 0)
+    attend(ring, 1)
+    gk.from_ring()
+    gv.from_ring()
+    gk.sib_ring()
+    gv.sib_ring()
+    attend_earlier(3, 0, 1)
+    attend_earlier(1, 0, 1)
+    gk.from_far()
+    gv.from_far()
+    gk.sib_far()
+    gv.sib_far()
+    attend_earlier(2, 1)
+    mean, log = far_part(1)
+    means[0] = mean
+    logs[0] = log.T[:8]
+    answers = [to_pair(1, means.at[0], means.at[1]), to_pair(2, logs.at[0], logs.at[1])]
+    for copy in answers:
+        copy.start()
+    attend_earlier(2, 0)
+    finish(mine, *far_part(0))
+    for copy in answers:
+        copy.wait_recv()
+    finish(theirs, means[1], jnp.broadcast_to(logs[1, 0:1, :], (HD, nslot)).T)
 
     for gather in (ga, gx, ge, gm, gk, gv):
         gather.finish()
-    for copy in straight + shared:
+    for copy in straight + shared + [asking] + answers:
         copy.wait_send()
 
 
@@ -610,7 +593,7 @@
         pltpu.VMEM((ntp, arows, wide), BF),
         pltpu.VMEM((ntp * arows, wide), BF),
         pltpu.VMEM((3, wide, hcols), BF),
-        pltpu.VMEM((nslot * chunks, HD), F32),
+        pltpu.VMEM((nchosen * chunks, HD), F32),
         pltpu.VMEM((nchosen, chunks, HD), BF),
         pltpu.VMEM((nseq, cap, chunks, HD), BF),
         pltpu.VMEM((ntp, nseq, cap, chunks, HD), BF),
@@ -619,14 +602,19 @@
         pltpu.VMEM((nseq, ntp * arows, ecols), BF),
         pltpu.VMEM((3, nslot, hcols), F32),
         pltpu.VMEM((ntp, 8, nslot), F32),
-        pltpu.VMEM((nslot, hcols), BF),
-        pltpu.VMEM((nseq, hcols + 16, nslot), BF),
-        pltpu.VMEM((nseq, nslot, hcols), BF),
+        pltpu.VMEM((heads, nslot, HD), BF),
+        pltpu.VMEM((heads, HD + 16, nslot), BF),
+        pltpu.VMEM((heads, nslot, HD), BF),
+        pltpu.VMEM((2, nslot, HD), BF),
+        pltpu.VMEM((nseq, HD + 16, nslot), BF),
+        pltpu.VMEM((nseq, nslot, HD), BF),
+        pltpu.VMEM((2, nslot, HD), BF),
+        pltpu.VMEM((2, 8, nslot), F32),
         pltpu.VMEM((npos, nslot), BF),
         pltpu.VMEM((nslot, npos), BF),
-        pltpu.VMEM((npos, hcols), BF),
-        pltpu.VMEM((hcols, npos), BF),
-        pltpu.VMEM((npos, hcols), BF),
+        pltpu.VMEM((npos, HD), BF),
+        pltpu.VMEM((HD, npos), BF),
+        pltpu.VMEM((npos, HD), BF),
         pltpu.VMEM((heads, npos, HD), F32),
         pltpu.VMEM((heads, npos, HD), F32),
         pltpu.VMEM((heads, nslot, HD), F32),
@@ -642,14 +630,16 @@
         dma((9,)),
         dma((17,)),
         dma((17,)),
-        dma((16,)),
-        dma((16,)),
+        dma((17,)),
+        dma((17,)),
         dma((ntp,)),
         dma((ntp,)),
         dma((17,)),
         dma((17,)),
-        dma((16,)),
-        dma((16,)),
+        dma((17,)),
+        dma((17,)),
+        dma((3,)),
+        dma((3,)),
     ]
     return pl.pallas_call(
         kernel,

time: 99.4 us -> 90.9 us (0.914)
  Pallas kernels: 97.3 us -> 88.8 us
    pallas_call x1, Pallas kernels: 97.3 us -> 88.8 us  [per_device(): pl.pallas_call(kernel, out_shape=jax.ShapeDtypeStruct((npos, hcols), BF),...]
where the time goes in v3:
time: 90.9 us; the launch traced here: 90.7 us
  Pallas kernels  88.8 us (98%)
  local copies, waits for them, and re-layouts  1.87 us (2%)
    pallas_call x1, Pallas kernels, per_device(): pl.pallas_call(kernel, out_shape=jax.ShapeDtypeStruct((npos, hcols), BF),...  88.8 us
    unnamed x1, local copies, waits for them, and re-layouts  1.87 us

profile of v3, /device:TPU:6, one launch (start us, length us, event | category | flops | bytes accessed | tf_op | source)
XLA Modules:
  0.0 90.7 jit_solution(3211998266790284011)
XLA Ops:
  0.0 88.8 %shard_map.100 = bf16[1024,256]{1,0:T(8,128)(2,1)} custom-call(s32[4]{0:T(128)} %lengths.1, bf16[256,2048]{1,0:T(8,128)(2,1)} %items.1, f32[1,2048]{1,0:T(1,128)} %bitcast.7, bf16[16,4096]{1,0:T(8,128)(2,1)} %adapter.1, s32[4,16]{1,0:T(4,128)} %bitcast.9, s32[8,128]{1,0:T(8,128)} %bitcast.8, f32[1,4096]{1,0:T(1,128)} %bitcast.6, bf16[4096,256]{1,0:T(8,128)(2,1)} %w_query.1, ...), custom_call_target="tpu_custom_call" | custom-call | tf_op jit(solution)/shard_map/pallas_call | solution.py:644
  88.8 1.9 %copy.12 = bf16[1024,256]{1,0:T(8,128)(2,1)} copy(bf16[1024,256]{1,0:T(8,128)(2,1)} %shard_map.100) | data formatting | bytes 1048576

commit v4 on v3

--- a/solution.py
+++ b/solution.py
@@ -42,12 +42,12 @@
 
 
 class Gather:
-    def __init__(self, group, buf, half, send, recv):
-        self.g, self.buf, self.half, self.send, self.recv = group, buf, half, send, recv
+    def __init__(self, group, base, half, send, recv):
+        self.g, self.base, self.half, self.send, self.recv = group, base, half, send, recv
         self.count, self.sent = 0, []
 
     def view(self, index, part=None):
-        ref = self.buf.at[index]
+        ref = self.base(index)
         if part is None:
             return ref
         axis, cut, end = self.half
@@ -103,9 +103,9 @@
         if g.cores:
             self.push(block, g.sib, 10)
 
-    def from_ring(self):
-        g = self.g
-        for dp in (0, 1):
+    def from_ring(self, dps=(0, 1)):
+        g = self.g
+        for dp in dps:
             block = g.block(3, dp)
             self.got(block, 1 + dp)
             self.push(block, g.right, 5 + dp, 0)
@@ -138,6 +138,80 @@
     def sib_far(self):
         for dp in (0, 1):
             self.got(self.g.block(2, dp, 1), 15 + dp)
+
+
+class RingFirst(Gather):
+    def start(self):
+        g = self.g
+        own = g.block()
+        self.push(own, g.right, 1)
+        self.push(own, g.left, 2)
+        self.push(own, g.pair, 0)
+        if g.cores:
+            self.push(own, g.sib, 8)
+
+    def from_pair(self):
+        g = self.g
+        block = g.block(0, 1)
+        self.got(block, 0)
+        if g.cores:
+            self.push(block, g.sib, 9)
+
+    def from_ring(self):
+        g = self.g
+        block = g.block(3, 0)
+        self.got(block, 1)
+        self.push(block, g.right, 3, 0)
+        self.push(block, g.pair, 5)
+        if g.cores:
+            self.push(block, g.sib, 10)
+        block = g.block(1, 0)
+        self.got(block, 2)
+        self.push(block, g.left, 4, 1)
+        self.push(block, g.pair, 6)
+        if g.cores:
+            self.push(block, g.sib, 11)
+
+    def from_far(self):
+        g = self.g
+        block = g.block(2, 0)
+        self.got(block, 3, 0)
+        self.got(block, 4, 1)
+        self.push(block, g.pair, 7)
+        if g.cores:
+            self.push(block, g.sib, 12)
+
+    def pair_ring(self):
+        g = self.g
+        for dr, slot in ((3, 5), (1, 6)):
+            block = g.block(dr, 1)
+            self.got(block, slot)
+            if g.cores:
+                self.push(block, g.sib, 8 + slot)
+
+    def pair_far(self):
+        g = self.g
+        block = g.block(2, 1)
+        self.got(block, 7)
+        if g.cores:
+            self.push(block, g.sib, 15)
+
+    def sib_own(self):
+        g = self.g
+        self.got(g.block(0, 0, 1), 8)
+        self.got(g.block(0, 1, 1), 9)
+
+    def sib_ring(self):
+        g = self.g
+        self.got(g.block(3, 0, 1), 10)
+        self.got(g.block(1, 0, 1), 11)
+        self.got(g.block(3, 1, 1), 13)
+        self.got(g.block(1, 1, 1), 14)
+
+    def sib_far(self):
+        g = self.g
+        self.got(g.block(2, 0, 1), 12)
+        self.got(g.block(2, 1, 1), 15)
 
 
 def pieces(values):
@@ -163,7 +237,6 @@
     weights,
     spread,
     xs,
-    xa,
     xb,
     rows,
     mix,
@@ -190,6 +263,8 @@
     w_sem,
     a_send,
     a_recv,
+    b_send,
+    b_recv,
     r_send,
     r_recv,
     c_send,
@@ -198,6 +273,10 @@
     x_recv,
     m_send,
     m_recv,
+    n_send,
+    n_recv,
+    o_send,
+    o_recv,
     e_send,
     e_recv,
     s_send,
@@ -254,8 +333,13 @@
     arows = adapter.shape[0]
 
     abuf[tp] = adapter[...]
-    ga = PairFirst(over_tp, abuf, (1, wide // 2, wide), a_send, a_recv)
+    cut = wide * 3 // 4
+    ga = PairFirst(over_tp, lambda i: abuf.at[i, :, :cut], (1, cut // 2, cut), a_send, a_recv)
+    ha = RingFirst(
+        over_tp, lambda i: abuf.at[i, :, cut:], (1, (wide - cut) // 2, wide - cut), b_send, b_recv
+    )
     ga.start()
+    ha.start()
 
     def columns_of(index):
         return adapter.at[:, pl.ds(pl.multiple_of(index * ecols, HD), ecols)]
@@ -270,13 +354,13 @@
             device_id_type=MESH,
         )
 
-    def routed_copy(k, peer, source):
+    def routed_copy(k, source):
         return pltpu.make_async_remote_copy(
-            src_ref=xs.at[pl.ds(peer * cap, cap)],
-            dst_ref=xa.at[source],
+            src_ref=xs.at[pl.ds(lax.rem(seq + k, nseq) * cap, cap)],
+            dst_ref=xb.at[tp, source],
             send_sem=r_send.at[k],
             recv_sem=r_recv.at[k],
-            device_id=(peer, tp),
+            device_id=(lax.rem(seq + k, nseq), tp),
             device_id_type=MESH,
         )
 
@@ -285,9 +369,9 @@
         straight.append(column_copy(k, lax.rem(tp + k, ntp), tp))
         straight[-1].start()
     for k in range(1, nseq):
-        straight.append(routed_copy(k, lax.rem(seq + k, nseq), seq))
+        straight.append(routed_copy(k, seq))
         straight[-1].start()
-    xa[seq] = xs[pl.ds(seq * cap, cap)]
+    xb[tp, seq] = xs[pl.ds(seq * cap, cap)]
     ebuf[seq, pl.ds(pl.multiple_of(tp * arows, arows), arows), :] = adapter[
         :, pl.ds(pl.multiple_of(tp * ecols, HD), ecols)
     ]
@@ -302,22 +386,24 @@
         place[here, :] = (lax.broadcasted_iota(jnp.int32, (HD, nslot), 1) == spot_t[:, k : k + 1]).astype(BF)
 
     ga.from_pair()
+    ha.from_ring()
     for k in range(1, ntp):
         column_copy(k, lax.rem(tp + k, ntp), lax.rem(tp + ntp - k, ntp)).wait_recv()
-    ge = PairFirst(over_seq, ebuf, (0, ntp * arows // 2, ntp * arows), e_send, e_recv)
+    ge = PairFirst(over_seq, lambda i: ebuf.at[i], (0, ntp * arows // 2, ntp * arows), e_send, e_recv)
     ge.start()
     for k in range(1, nseq):
-        routed_copy(k, lax.rem(seq + k, nseq), lax.rem(seq + nseq - k, nseq)).wait_recv()
-    xb[tp] = xa[...]
-    gx = PairFirst(over_tp, xb, (0, nseq // 2, nseq), x_send, x_recv)
+        routed_copy(k, lax.rem(seq + nseq - k, nseq)).wait_recv()
+    gx = PairFirst(over_tp, lambda i: xb.at[i], (0, nseq // 2, nseq), x_send, x_recv)
     gx.start()
     ga.from_ring()
-    ge.from_pair()
-
-    def lay_out(block):
+    ha.from_far()
+    ha.from_pair()
+
+    def lay_out(*block):
+        index = over_tp.block(*block)
         size = nchosen * chunks
-        spread[...] = xb[block].reshape(size, HD).astype(F32)
-        first = pl.multiple_of(block * nchosen, nchosen)
+        spread[...] = xb[index].reshape(size, HD).astype(F32)
+        first = pl.multiple_of(index * nchosen, nchosen)
         for k in range(chunks):
             piece = spread[pl.ds(k, nchosen, stride=chunks), :]
             rows[pl.ds(first, nchosen), k * HD : (k + 1) * HD] = piece.astype(BF)
@@ -346,29 +432,66 @@
     for h in range(heads):
         kown[h, HD:, :] = weigh.astype(BF)
 
+    ge.from_pair()
+    ha.pair_ring()
     ga.from_far()
+    ha.pair_far()
     arows = ntp * arows
     scaled[...] = (abuf[...].reshape(arows, wide).astype(F32) * user_gain[...]).astype(BF)
-    for i, load in enumerate(loads):
-        load.wait()
+
+    def part_of(i):
+        return lambda index: mix.at[index, :, pl.ds(i * hcols, hcols)]
+
+    def multiply(i):
+        loads[i].wait()
         mix[seq, :, i * hcols : (i + 1) * hcols] = dot(scaled[...], weights[i]).astype(BF)
-    gm = PairFirst(over_seq, mix, (0, arows // 2, arows), m_send, m_recv)
+
+    halves = (0, arows // 2, arows)
+    gq = PairFirst(over_seq, part_of(0), halves, m_send, m_recv)
+    gm = PairFirst(over_seq, part_of(1), halves, n_send, n_recv)
+    gw = RingFirst(over_seq, part_of(2), halves, o_send, o_recv)
+    multiply(1)
     gm.start()
-
     gx.from_pair()
+    multiply(2)
+    gw.start()
+    multiply(0)
+    gq.start()
+    lay_out()
+    lay_out(0, 1)
+    gm.from_pair()
     ge.from_ring()
-    lay_out(over_tp.block())
-    lay_out(over_tp.block(0, 1))
-    gm.from_pair()
+    gx.from_ring()
+    gq.from_pair()
+    gw.from_ring()
+    gw.from_pair()
+    for dp in (0, 1):
+        lay_out(3, dp)
+        lay_out(1, dp)
     ge.from_far()
-    gx.from_ring()
-    for dp in (0, 1):
-        lay_out(over_tp.block(3, dp))
-        lay_out(over_tp.block(1, dp))
     gm.from_ring()
+    gq.from_ring()
+    gw.from_far()
+    gw.pair_ring()
+    gm.from_far()
     gx.from_far()
     for dp in (0, 1):
-        lay_out(over_tp.block(2, dp))
+        lay_out(2, dp)
+
+    def project(i):
+        raw[i] = dot(rows[...], mix[:, :, i * hcols : (i + 1) * hcols].reshape(ditem, hcols))
+
+    mine = (seq // 2) % 2
+    theirs = 1 - mine
+    gm.sib_own()
+    gm.sib_ring()
+    gm.sib_far()
+    project(1)
+    for h in range(heads):
+        kown[h, :HD, :] = raw[1, :, h * HD : (h + 1) * HD].T.astype(BF)
+    kt[seq] = kown[mine]
+    gk = PairFirst(over_seq, lambda i: kt.at[i], (0, 64, kt.shape[1]), k_send, k_recv)
+    gk.start(kown.at[theirs])
     ge.sib_own()
     ge.sib_ring()
     ge.sib_far()
@@ -393,12 +516,15 @@
         )
         copy.start()
         shared.append(copy)
-    gm.from_far()
-    gm.sib_own()
-    gm.sib_ring()
-    gm.sib_far()
-    for i in range(3):
-        raw[i] = dot(rows[...], mix[:, :, i * hcols : (i + 1) * hcols].reshape(ditem, hcols))
+    gk.from_pair()
+    gk.from_ring((0,))
+    gq.from_far()
+    gw.pair_far()
+    for gather in (gw, gq):
+        gather.sib_own()
+        gather.sib_ring()
+        gather.sib_far()
+    project(2)
     for k in range(1, ntp):
         other = lax.rem(tp + ntp - k, ntp)
         pltpu.make_async_remote_copy(
@@ -414,18 +540,20 @@
         total = total + sums[k]
     inverse = lax.rsqrt(total[0:1, :] / wide + EPS)
     down = jnp.broadcast_to(inverse, (HD, nslot)).T
-    mine = (seq // 2) % 2
-    theirs = 1 - mine
     for h in range(heads):
-        kown[h, :HD, :] = (raw[1, :, h * HD : (h + 1) * HD].T * inverse).astype(BF)
-    kt[seq] = kown[mine]
-    gk = PairFirst(over_seq, kt, (0, 64, kt.shape[1]), k_send, k_recv)
-    gk.start(kown.at[theirs])
+        vown[h, :nslot] = (raw[2, :, h * HD : (h + 1) * HD] * down).astype(BF)
+    line = lax.broadcasted_iota(jnp.int32, (16, HD), 0)
+    tiles = nslot // HD
+    norms = jnp.zeros((16, HD), F32)
+    for r, term in enumerate(pieces(inverse)):
+        for k in range(tiles):
+            norms = jnp.where(line == r * tiles + k, term[:, k * HD : (k + 1) * HD], norms)
     for h in range(heads):
-        vown[h] = (raw[2, :, h * HD : (h + 1) * HD] * down).astype(BF)
+        vown[h, nslot:] = norms.astype(BF)
     val[seq] = vown[mine]
-    gv = PairFirst(over_seq, val, (0, nslot // 2, nslot), v_send, v_recv)
+    gv = PairFirst(over_seq, lambda i: val.at[i], (0, nslot // 2, val.shape[1]), v_send, v_recv)
     gv.start(vown.at[theirs])
+    project(0)
     for h in range(heads):
         query[h] = (raw[0, :, h * HD : (h + 1) * HD] * (down * (LOG2E / math.sqrt(HD)))).astype(BF)
 
@@ -447,8 +575,9 @@
 
     def attend_near(h):
         qpos[...] = dot(place[...], query[h]).astype(BF)
-        vpos[...] = dot(place[...], vown[h]).astype(BF)
-        kpos_t[...] = dot(kown[h, :HD, :], place_t[...]).astype(BF)
+        vpos[...] = dot(place[...], vown[h, :nslot]).astype(BF)
+        scaled_keys = (kown[h, :HD, :].astype(F32) * inverse).astype(BF)
+        kpos_t[...] = dot(scaled_keys, place_t[...]).astype(BF)
         for i in range(npos // step):
             here, upto = slice(i * step, (i + 1) * step), (i + 1) * step
             score = dot(qpos[here], kpos_t[:, :upto])
@@ -472,21 +601,31 @@
     def attend(ring, j):
         user_here = user_of(jnp.zeros((16, nslot), jnp.int32) + sides[j] * npos)
         chosen_rows = (which % USERS == user_here) & (which < 3 * USERS)
-        bias = []
+        bias, factor = [], []
         for i in range(4):
             tail = kt[ring * 4 + i, HD:, :].astype(F32)
-            line = jnp.sum(jnp.where(chosen_rows, tail, 0.0), axis=0, keepdims=True)
-            bias.append(jnp.where(jnp.zeros_like(line, jnp.int32) + ring * 4 + i < sides[j], line, EMPTY))
+            held = jnp.sum(jnp.where(chosen_rows, tail, 0.0), axis=0, keepdims=True)
+            bias.append(jnp.where(jnp.zeros_like(held, jnp.int32) + ring * 4 + i < sides[j], held, EMPTY))
+            tail = val[ring * 4 + i, nslot:, :].astype(F32)
+            factor.append(
+                jnp.concatenate(
+                    [
+                        jnp.sum(jnp.where((line % tiles == k) & (line < 3 * tiles), tail, 0.0), axis=0, keepdims=True)
+                        for k in range(tiles)
+                    ],
+                    axis=1,
+                )
+            )
         for b in range(nslot // band):
             here = slice(b * band, (b + 1) * band)
-            scores = [dot(asked[j, here], kt[ring * 4 + i, :HD, :]) + bias[i] for i in range(4)]
+            scores = [dot(asked[j, here], kt[ring * 4 + i, :HD, :]) * factor[i] + bias[i] for i in range(4)]
             largest = jnp.maximum(jnp.maximum(scores[0], scores[1]), jnp.maximum(scores[2], scores[3]))
             before = top[j, here]
             after = jnp.maximum(before, jnp.max(largest, axis=1, keepdims=True))
             both = None
             for i in range(4):
                 prob = jnp.exp2(scores[i] - after[:, :1]).astype(BF)
-                part = dot(prob, jnp.concatenate([val[ring * 4 + i], ones], axis=1))
+                part = dot(prob, jnp.concatenate([val[ring * 4 + i, :nslot], ones], axis=1))
                 both = part if both is None else both + part
             shrink = jnp.exp2(before - after)
             accum[j, here] = accum[j, here] * jnp.concatenate([shrink, shrink], axis=1) + both
@@ -525,22 +664,23 @@
 
     ring = seq // 4
     attend_near(0)
-    gk.from_pair()
+    gk.from_ring((1,))
+    attend_near(1)
     gv.from_pair()
-    attend_near(1)
+    gv.from_ring((0,))
     asking.wait_recv()
     gk.sib_own()
     gv.sib_own()
+    attend(ring, 1)
     attend(ring, 0)
-    attend(ring, 1)
-    gk.from_ring()
-    gv.from_ring()
+    gv.from_ring((1,))
     gk.sib_ring()
     gv.sib_ring()
-    attend_earlier(3, 0, 1)
-    attend_earlier(1, 0, 1)
+    attend_earlier(3, 1)
+    attend_earlier(1, 1)
     gk.from_far()
     gv.from_far()
+    attend_earlier(3, 0)
     gk.sib_far()
     gv.sib_far()
     attend_earlier(2, 1)
@@ -550,13 +690,14 @@
     answers = [to_pair(1, means.at[0], means.at[1]), to_pair(2, logs.at[0], logs.at[1])]
     for copy in answers:
         copy.start()
+    attend_earlier(1, 0)
     attend_earlier(2, 0)
     finish(mine, *far_part(0))
     for copy in answers:
         copy.wait_recv()
     finish(theirs, means[1], jnp.broadcast_to(logs[1, 0:1, :], (HD, nslot)).T)
 
-    for gather in (ga, gx, ge, gm, gk, gv):
+    for gather in (ga, ha, gx, ge, gq, gm, gw, gk, gv):
         gather.finish()
     for copy in straight + shared + [asking] + answers:
         copy.wait_send()
@@ -595,7 +736,6 @@
         pltpu.VMEM((3, wide, hcols), BF),
         pltpu.VMEM((nchosen * chunks, HD), F32),
         pltpu.VMEM((nchosen, chunks, HD), BF),
-        pltpu.VMEM((nseq, cap, chunks, HD), BF),
         pltpu.VMEM((ntp, nseq, cap, chunks, HD), BF),
         pltpu.VMEM((nslot, ditem), BF),
         pltpu.VMEM((nseq, ntp * arows, 3 * hcols), BF),
@@ -604,10 +744,10 @@
         pltpu.VMEM((ntp, 8, nslot), F32),
         pltpu.VMEM((heads, nslot, HD), BF),
         pltpu.VMEM((heads, HD + 16, nslot), BF),
-        pltpu.VMEM((heads, nslot, HD), BF),
+        pltpu.VMEM((heads, nslot + 16, HD), BF),
         pltpu.VMEM((2, nslot, HD), BF),
         pltpu.VMEM((nseq, HD + 16, nslot), BF),
-        pltpu.VMEM((nseq, nslot, HD), BF),
+        pltpu.VMEM((nseq, nslot + 16, HD), BF),
         pltpu.VMEM((2, nslot, HD), BF),
         pltpu.VMEM((2, 8, nslot), F32),
         pltpu.VMEM((npos, nslot), BF),
@@ -622,6 +762,8 @@
         dma((3,)),
         dma((9,)),
         dma((9,)),
+        dma((8,)),
+        dma((8,)),
         dma((nseq,)),
         dma((nseq,)),
         dma((ntp,)),
@@ -630,6 +772,10 @@
         dma((9,)),
         dma((17,)),
         dma((17,)),
+        dma((17,)),
+        dma((17,)),
+        dma((16,)),
+        dma((16,)),
         dma((17,)),
         dma((17,)),
         dma((ntp,)),

time: 90.9 us -> 89.7 us (0.987)
  Pallas kernels: 88.8 us -> 87.2 us
    pallas_call x1, Pallas kernels: 88.8 us -> 87.2 us  [per_device(): pl.pallas_call(kernel, out_shape=jax.ShapeDtypeStruct((npos, hcols), BF),...]
where the time goes in v4:
time: 89.7 us; the launch traced here: 89.1 us
  Pallas kernels  87.2 us (97%)
  local copies, waits for them, and re-layouts  1.87 us (2%)
    pallas_call x1, Pallas kernels, per_device(): pl.pallas_call(kernel, out_shape=jax.ShapeDtypeStruct((npos, hcols), BF),...  87.2 us
    unnamed x1, local copies, waits for them, and re-layouts  1.87 us

profile of v4, /device:TPU:6, one launch (start us, length us, event | category | flops | bytes accessed | tf_op | source)
XLA Modules:
  0.0 89.1 jit_solution(12251247856144884271)
XLA Ops:
  0.0 87.2 %shard_map.100 = bf16[1024,256]{1,0:T(8,128)(2,1)} custom-call(s32[4]{0:T(128)} %lengths.1, bf16[256,2048]{1,0:T(8,128)(2,1)} %items.1, f32[1,2048]{1,0:T(1,128)} %bitcast.7, bf16[16,4096]{1,0:T(8,128)(2,1)} %adapter.1, s32[4,16]{1,0:T(4,128)} %bitcast.9, s32[8,128]{1,0:T(8,128)} %bitcast.8, f32[1,4096]{1,0:T(1,128)} %bitcast.6, bf16[4096,256]{1,0:T(8,128)(2,1)} %w_query.1, ...), custom_call_target="tpu_custom_call" | custom-call | tf_op jit(solution)/shard_map/pallas_call | solution.py:790
  87.2 1.9 %copy.12 = bf16[1024,256]{1,0:T(8,128)(2,1)} copy(bf16[1024,256]{1,0:T(8,128)(2,1)} %shard_map.100) | data formatting | bytes 1048576
